TPU v7x, 256 devices: a whole 4x4x8 slice. The times are simulated.
256 devices in a mesh: seq: 32 (over y_hi, z, core), grp: 8 (over x, y_lo).
Axes of the slice: x: 4, y: 4 (y_hi: 2, y_lo: 2; y = y_hi * 2 + y_lo), z: 8, core: 2. Of those that a mesh axis runs over, the one named last changes fastest.
Arguments:
- units: bfloat16 [32768, 1024], P(('grp', 'seq')), parts along dimension 0, may hold values from -6 to 6
- durations: int32 [32768], P(('grp', 'seq')), parts along dimension 0, may hold values from 1 to 12, 24576 in all
- seg_ids: int32 [32768], P(('grp', 'seq')), parts along dimension 0, may hold values from 0 to 7, never falling along the last dimension, each value on 1 to 2048 neighbouring positions
- ln_gain: float32 [1024], replicated, may hold values from 0.1 to 1.9
- w_qkv: bfloat16 [1024, 3072], replicated, may hold values from -8 to 8
- w_out: bfloat16 [1024, 1024], replicated, may hold values from -0.1875 to 0.1875
- w_proj: bfloat16 [1024, 512], replicated, may hold values from -0.1875 to 0.1875
- conv_w: bfloat16 [5, 512, 512], replicated, may hold values from -0.125 to 0.125
- conv_b: float32 [512], replicated, may hold values from -3 to 3
- conv_gain: float32 [512], replicated, may hold values from 0.1 to 1.9
Outputs:
- frames_out: bfloat16 [196608, 512], P(('grp', 'seq')), parts along dimension 0
There are 8 independent parts, one for each index of `grp`. A program takes and returns all parts, laid end to end along the dimension named above; an argument that names none is the same for every part. Nothing has to cross between parts.
All inputs are finite; a program needn't handle non-finite values. No bound on the sum of `durations` on one device may be relied on, other than what follows from the above.
Results may differ from a plain program's by a relative error of at most 0.0098.
Values may be sent and summed in bfloat16 or wider, within the bound.
A program may use at most 128 MiB of HBM per device.

v0:
```python
import jax
import jax.numpy as jnp
from jax import lax
from jax.sharding import PartitionSpec as P

HEADS = 16
KERNEL = 5
DUR_MEAN = 6


def extended(array, sides, width):
    for axis, dim in sides:
        size, length = (lax.axis_size(axis), array.shape[dim])
        up = [(i, (i + 1) % size) for i in range(size - 1)]
        down = [(j, i) for i, j in up]
        last = lax.slice_in_dim(array, length - width, length, axis=dim)
        initial = lax.slice_in_dim(array, 0, width, axis=dim)
        before = lax.ppermute(last, axis, up)
        after = lax.ppermute(initial, axis, down)
        array = jnp.concatenate([before, array, after], axis=dim)
    return array


def normalize(values, gain):
    mean = jnp.mean(values, axis=-1, keepdims=True)
    centred = values - mean
    variance = jnp.mean(centred * centred, axis=-1, keepdims=True)
    return centred / jnp.sqrt(variance + 1e-05) * gain


def local(units, durations, seg_ids, ln_gain, w_qkv, w_out, w_proj, conv_w, conv_b, conv_gain):
    n_units = units.shape[0]
    width = units.shape[1]
    head_size = width // HEADS
    scale = 1.0 / jnp.sqrt(jnp.float32(head_size))
    x = units.astype(jnp.float32)
    h = normalize(x, ln_gain).astype(jnp.bfloat16)
    query = jnp.dot(h, w_qkv[:, :width], preferred_element_type=jnp.float32).astype(jnp.bfloat16)
    query = query.reshape(n_units, HEADS, head_size)
    seg_query = seg_ids.astype(jnp.float32)
    seg_wire = seg_ids.astype(jnp.bfloat16)
    start_top = jnp.full((HEADS, n_units), -1e30, jnp.float32)
    kv_local = jnp.dot(h, w_qkv[:, width:], preferred_element_type=jnp.float32).astype(jnp.bfloat16)
    kv_rows = lax.all_gather(kv_local, "seq", axis=0, tiled=True)
    top = start_top
    count = kv_rows.shape[0]
    keys = kv_rows[:, :width].reshape(count, HEADS, head_size)
    values = kv_rows[:, width:].reshape(count, HEADS, head_size)
    allowed = (
        seg_query[:, None]
        == lax.all_gather(seg_wire, "seq", axis=0, tiled=True).astype(jnp.float32)[None, :]
    )[None]
    scores = jnp.einsum("qhd,khd->hqk", query, keys, preferred_element_type=jnp.float32) * scale
    scores = jnp.where(allowed, scores, jnp.float32(-1e30))
    new_top = jnp.maximum(top, jnp.max(scores, axis=2))
    expo = jnp.where(allowed, jnp.exp(scores - new_top[:, :, None]), jnp.float32(0.0))
    total = jnp.sum(expo, axis=2)
    acc = jnp.einsum(
        "hqk,khd->hqd", expo.astype(jnp.bfloat16), values, preferred_element_type=jnp.float32
    )
    acc, top, total = (acc, new_top, total)
    heads_out = acc / total[:, :, None]
    attended = heads_out.transpose(1, 0, 2).reshape(n_units, width).astype(jnp.bfloat16)
    mixed = (jnp.dot(attended, w_out, preferred_element_type=jnp.float32) + x).astype(jnp.bfloat16)
    reduced = jnp.dot(mixed, w_proj, preferred_element_type=jnp.float32).astype(jnp.bfloat16)
    whole_reduced, whole_dur = (
        lax.all_gather(reduced, "seq", axis=0, tiled=True),
        lax.all_gather(durations.astype(jnp.bfloat16), "seq", axis=0, tiled=True),
    )
    ends = jnp.cumsum(whole_dur.astype(jnp.int32))
    frame_count = DUR_MEAN * n_units
    first_frame = lax.axis_index("seq") * frame_count
    frame_pos = first_frame + jnp.arange(frame_count, dtype=jnp.int32)
    unit_of = jnp.searchsorted(ends, frame_pos, side="right")
    expanded = jnp.take(whole_reduced, unit_of, axis=0)
    half = KERNEL // 2
    padded = extended(expanded, (("seq", 0),), half)
    conv = jnp.zeros((frame_count, expanded.shape[1]), jnp.float32) + conv_b
    for tap in range(KERNEL):
        conv = conv + jnp.dot(
            padded[tap : tap + frame_count], conv_w[tap], preferred_element_type=jnp.float32
        )
    result = expanded.astype(jnp.float32) + normalize(jax.nn.relu(conv), conv_gain)
    return result.astype(jnp.bfloat16)


def solution(mesh):
    in_specs = (
        P(("grp", "seq"), None),
        P(("grp", "seq")),
        P(("grp", "seq")),
        P(),
        P(),
        P(),
        P(),
        P(),
        P(),
        P(),
    )
    out_specs = P(("grp", "seq"), None)
    return jax.shard_map(local, mesh=mesh, in_specs=in_specs, out_specs=out_specs, check_vma=False)
```

profile of v0, /device:TPU:1, one launch (start us, length us, event | category | flops | bytes accessed | tf_op | source)
XLA Modules:
  0.0 354.1 jit_solution(14908280064859130744)
XLA Ops:
  9.0 3.9 %fusion.10 = bf16[128,2048]{1,0:T(8,128)(2,1)} fusion(bf16[1024,3072]{1,0:T(8,128)(2,1)} %param.16, bf16[128,1024]{1,0:T(8,128)(2,1)} %param.12, f32[1024]{0:T(1024)} %param.15, f32[128]{0:T(128)S(1)} %add_sqrt_fusion.1, f32[128]{0:T(128)S(1)} %broadcast_multiply_fusion.1), kind=kOutput, calls=%fused_computation.17 | convolution fusion | flops 537788416 | bytes 4985856 | tf_op jit(solution)/shard_map/dot_general | solution.py:43
  13.0 46.0 %all-gather.1 = bf16[32,1,128]{2,1,0:T(2,128)(2,1)S(1)} all-gather(bf16[1,1,128]{2,1,0:T(2,128)(2,1)S(1)} %get-tuple-element.109), channel_id=1, replica_groups=mesh['seq'=32,'grp'=8] {'seq'}, dimensions={0}, use_global_device_ids=true | all-gather | bytes 8448 | tf_op jit(solution)/shard_map/all_gather | solution.py:51
  59.1 2.1 fusion.18
  61.4 36.5 %all-gather = bf16[32,1,128]{2,1,0:T(2,128)(2,1)S(1)} all-gather(bf16[1,1,128]{2,1,0:T(2,128)(2,1)S(1)} %convert_bitcast_fusion.1), channel_id=1, replica_groups=mesh['seq'=32,'grp'=8] {'seq'}, dimensions={0}, use_global_device_ids=true | all-gather | bytes 8448 | tf_op jit(solution)/shard_map/all_gather | solution.py:68
  98.9 56.1 %all-gather.5.cloned.1.call-done = bf16[4096,2048]{1,0:T(8,128)(2,1)} async-done(((bf16[128,2048]{1,0:T(8,128)(2,1)}), bf16[4096,2048]{1,0:T(8,128)(2,1)}) %all-gather.5.cloned.1.call-update) | async-done | bytes 16777232 | tf_op jit(solution)/shard_map/all_gather | solution.py:44
  155.0 11.6 %fusion.66 = (bf16[4096,1024]{1,0:T(8,128)(2,1)}, bf16[4096,1024]{1,0:T(8,128)(2,1)}) fusion(bf16[4096,2048]{1,0:T(8,128)(2,1)} %all-gather.5.cloned.1.call-done), kind=kLoop, calls=%fused_computation.85 | loop fusion | bytes 33554432 | tf_op jit(solution)/shard_map/slice | solution.py:47
  166.6 11.4 %copy.23 = bf16[4096,1024]{0,1:T(8,128)(2,1)} copy(bf16[4096,1024]{1,0:T(8,128)(2,1)} %get-tuple-element.105) | data formatting | bytes 16777216 | tf_op jit(solution)/shard_map/slice | solution.py:48
  178.0 11.7 %copy.22 = bf16[4096,1024]{0,1:T(8,128)(2,1)} copy(bf16[4096,1024]{1,0:T(8,128)(2,1)} %get-tuple-element.104) | data formatting | bytes 16777216 | tf_op jit(solution)/shard_map/slice | solution.py:47
  189.7 15.8 %fusion.2 = (f32[16,128]{1,0:T(8,128)S(1)}, f32[16,128,4096]{2,1,0:T(8,128)}) fusion(pred[128,4096]{1,0:T(8,128)(4,1)S(1)} %broadcast_compare_fusion, bf16[128,16,64]{0,2,1:T(8,128)(2,1)S(1)} %bitcast.45, bf16[4096,16,64]{0,2,1:T(8,128)(2,1)} %bitcast.43), kind=kOutput, calls=%fused_computation.10 | convolution fusion | flops 1098905600 | bytes 42737664 | tf_op jit(solution)/shard_map/qhd,khd->hqk/dot_general | solution.py:53
  205.5 15.9 %fusion.3 = f32[16,128]{1,0:T(8,128)S(1)} fusion(f32[16,128,4096]{2,1,0:T(8,128)} %get-tuple-element.111, f32[16,128]{1,0:T(8,128)S(1)} %broadcast_maximum_fusion, pred[128,4096]{1,0:T(8,128)(4,1)S(1)} %broadcast_compare_fusion), kind=kLoop, calls=%fused_computation.11 | loop fusion | flops 41940992 | bytes 34095104 | tf_op jit(solution)/shard_map/reduce_sum | solution.py:57
  221.4 16.8 %fusion.27 = bf16[128,16,64]{0,2,1:T(8,128)(2,1)S(1)} fusion(bf16[4096,16,64]{0,2,1:T(8,128)(2,1)} %bitcast.44, f32[16,128,4096]{2,1,0:T(8,128)} %get-tuple-element.111, f32[16,128]{1,0:T(8,128)S(1)} %broadcast_maximum_fusion, pred[128,4096]{1,0:T(8,128)(4,1)S(1)} %broadcast_compare_fusion, f32[128,16]{0,1:T(8,128)S(1)} %bitcast.49), kind=kOutput, calls=%fused_computation.35 | convolution fusion | flops 1115947008 | bytes 42745856 | tf_op jit(solution)/shard_map/hqk,khd->hqd/dot_general | solution.py:58
  238.2 2.6 fusion.23
  240.8 59.3 %while.24 = (s32[]{:T(128)}, u32[768]{0:T(1024)S(1)}, u32[768]{0:T(1024)S(1)}, s32[4096]{0:T(1024)S(1)}, s32[]{:T(128)}, /*index=5*/s32[]{:T(128)}, s32[]{:T(128)}, s32[]{}) while((s32[]{:T(128)}, u32[768]{0:T(1024)S(1)}, u32[768]{0:T(1024)S(1)}, s32[4096]{0:T(1024)S(1)}, s32[]{:T(128)}, /*index=5*/s32[]{:T(128)}, s32[]{:T(128)}, ...), condition=%wide.region_3.4_spmd.clone, body=%wide.region_2.3_spmd.clone.sunk | while | flops 15620 | bytes 54905 | solution.py:74
  240.8 4.5 %gather_fusion = s32[768]{0:T(1024)S(1)} fusion(s32[4096]{0:T(1024)S(1)} %get-tuple-element.168, u32[1024]{0:T(1024)S(1)} %pad_clamp_fusion.3), kind=kCustom, calls=%fused_computation.clone.clone.1 | custom fusion | bytes 9216 | tf_op jit(solution)/shard_map/jit(searchsorted)/jit(_searchsorted_scan_impl)/vmap(jit(_searchsorted_scan_impl))/while/body/eval_jaxpr/gather | solution.py:74
  245.4 4.5 %gather_fusion = s32[768]{0:T(1024)S(1)} fusion(s32[4096]{0:T(1024)S(1)} %get-tuple-element.168, u32[1024]{0:T(1024)S(1)} %pad_clamp_fusion.3), kind=kCustom, calls=%fused_computation.clone.clone.1 | custom fusion | bytes 9216 | tf_op jit(solution)/shard_map/jit(searchsorted)/jit(_searchsorted_scan_impl)/vmap(jit(_searchsorted_scan_impl))/while/body/eval_jaxpr/gather | solution.py:74
  250.0 4.5 %gather_fusion = s32[768]{0:T(1024)S(1)} fusion(s32[4096]{0:T(1024)S(1)} %get-tuple-element.168, u32[1024]{0:T(1024)S(1)} %pad_clamp_fusion.3), kind=kCustom, calls=%fused_computation.clone.clone.1 | custom fusion | bytes 9216 | tf_op jit(solution)/shard_map/jit(searchsorted)/jit(_searchsorted_scan_impl)/vmap(jit(_searchsorted_scan_impl))/while/body/eval_jaxpr/gather | solution.py:74
  254.5 4.5 %gather_fusion = s32[768]{0:T(1024)S(1)} fusion(s32[4096]{0:T(1024)S(1)} %get-tuple-element.168, u32[1024]{0:T(1024)S(1)} %pad_clamp_fusion.3), kind=kCustom, calls=%fused_computation.clone.clone.1 | custom fusion | bytes 9216 | tf_op jit(solution)/shard_map/jit(searchsorted)/jit(_searchsorted_scan_impl)/vmap(jit(_searchsorted_scan_impl))/while/body/eval_jaxpr/gather | solution.py:74
  259.1 4.5 %gather_fusion = s32[768]{0:T(1024)S(1)} fusion(s32[4096]{0:T(1024)S(1)} %get-tuple-element.168, u32[1024]{0:T(1024)S(1)} %pad_clamp_fusion.3), kind=kCustom, calls=%fused_computation.clone.clone.1 | custom fusion | bytes 9216 | tf_op jit(solution)/shard_map/jit(searchsorted)/jit(_searchsorted_scan_impl)/vmap(jit(_searchsorted_scan_impl))/while/body/eval_jaxpr/gather | solution.py:74
  263.6 4.5 %gather_fusion = s32[768]{0:T(1024)S(1)} fusion(s32[4096]{0:T(1024)S(1)} %get-tuple-element.168, u32[1024]{0:T(1024)S(1)} %pad_clamp_fusion.3), kind=kCustom, calls=%fused_computation.clone.clone.1 | custom fusion | bytes 9216 | tf_op jit(solution)/shard_map/jit(searchsorted)/jit(_searchsorted_scan_impl)/vmap(jit(_searchsorted_scan_impl))/while/body/eval_jaxpr/gather | solution.py:74
  268.2 4.5 %gather_fusion = s32[768]{0:T(1024)S(1)} fusion(s32[4096]{0:T(1024)S(1)} %get-tuple-element.168, u32[1024]{0:T(1024)S(1)} %pad_clamp_fusion.3), kind=kCustom, calls=%fused_computation.clone.clone.1 | custom fusion | bytes 9216 | tf_op jit(solution)/shard_map/jit(searchsorted)/jit(_searchsorted_scan_impl)/vmap(jit(_searchsorted_scan_impl))/while/body/eval_jaxpr/gather | solution.py:74
  272.8 4.5 %gather_fusion = s32[768]{0:T(1024)S(1)} fusion(s32[4096]{0:T(1024)S(1)} %get-tuple-element.168, u32[1024]{0:T(1024)S(1)} %pad_clamp_fusion.3), kind=kCustom, calls=%fused_computation.clone.clone.1 | custom fusion | bytes 9216 | tf_op jit(solution)/shard_map/jit(searchsorted)/jit(_searchsorted_scan_impl)/vmap(jit(_searchsorted_scan_impl))/while/body/eval_jaxpr/gather | solution.py:74
  277.3 4.5 %gather_fusion = s32[768]{0:T(1024)S(1)} fusion(s32[4096]{0:T(1024)S(1)} %get-tuple-element.168, u32[1024]{0:T(1024)S(1)} %pad_clamp_fusion.3), kind=kCustom, calls=%fused_computation.clone.clone.1 | custom fusion | bytes 9216 | tf_op jit(solution)/shard_map/jit(searchsorted)/jit(_searchsorted_scan_impl)/vmap(jit(_searchsorted_scan_impl))/while/body/eval_jaxpr/gather | solution.py:74
  281.9 4.5 %gather_fusion = s32[768]{0:T(1024)S(1)} fusion(s32[4096]{0:T(1024)S(1)} %get-tuple-element.168, u32[1024]{0:T(1024)S(1)} %pad_clamp_fusion.3), kind=kCustom, calls=%fused_computation.clone.clone.1 | custom fusion | bytes 9216 | tf_op jit(solution)/shard_map/jit(searchsorted)/jit(_searchsorted_scan_impl)/vmap(jit(_searchsorted_scan_impl))/while/body/eval_jaxpr/gather | solution.py:74
  286.4 4.5 %gather_fusion = s32[768]{0:T(1024)S(1)} fusion(s32[4096]{0:T(1024)S(1)} %get-tuple-element.168, u32[1024]{0:T(1024)S(1)} %pad_clamp_fusion.3), kind=kCustom, calls=%fused_computation.clone.clone.1 | custom fusion | bytes 9216 | tf_op jit(solution)/shard_map/jit(searchsorted)/jit(_searchsorted_scan_impl)/vmap(jit(_searchsorted_scan_impl))/while/body/eval_jaxpr/gather | solution.py:74
  291.0 4.5 %gather_fusion = s32[768]{0:T(1024)S(1)} fusion(s32[4096]{0:T(1024)S(1)} %get-tuple-element.168, u32[1024]{0:T(1024)S(1)} %pad_clamp_fusion.3), kind=kCustom, calls=%fused_computation.clone.clone.1 | custom fusion | bytes 9216 | tf_op jit(solution)/shard_map/jit(searchsorted)/jit(_searchsorted_scan_impl)/vmap(jit(_searchsorted_scan_impl))/while/body/eval_jaxpr/gather | solution.py:74
  295.6 4.5 %gather_fusion = s32[768]{0:T(1024)S(1)} fusion(s32[4096]{0:T(1024)S(1)} %get-tuple-element.168, u32[1024]{0:T(1024)S(1)} %pad_clamp_fusion.3), kind=kCustom, calls=%fused_computation.clone.clone.1 | custom fusion | bytes 9216 | tf_op jit(solution)/shard_map/jit(searchsorted)/jit(_searchsorted_scan_impl)/vmap(jit(_searchsorted_scan_impl))/while/body/eval_jaxpr/gather | solution.py:74
  300.1 24.3 %all-gather.7.cloned.1.call-done = bf16[4096,512]{1,0:T(8,128)(2,1)} async-done(((bf16[128,512]{1,0:T(8,128)(2,1)}), bf16[4096,512]{1,0:T(8,128)(2,1)}) %all-gather.7.cloned.1.call-update) | async-done | bytes 4194320 | tf_op jit(solution)/shard_map/all_gather | solution.py:67
  324.5 6.1 %gather_fusion.1 = bf16[768,512]{1,0:T(8,128)(2,1)} fusion(bf16[4096,512]{1,0:T(8,128)(2,1)} %all-gather.7.cloned.1.call-done, s32[1024]{0:T(1024)S(1)} %pad_clamp_fusion.1), kind=kCustom, calls=%fused_computation.1 | custom fusion | bytes 1575936 | tf_op jit(solution)/shard_map/jit(_take)/gather | solution.py:75
  332.2 2.5 collective-permute-start.1
  334.7 3.4 collective-permute-start
  338.1 1.7 fusion.48
  345.0 2.3 copy.25
  (119 shorter events, 10.9 us)
Async XLA Ops:
  6.5 231.7 %copy-start = (bf16[1024,1024]{1,0:T(8,128)(2,1)S(1)}, bf16[1024,1024]{1,0:T(8,128)(2,1)}, u32[]{:S(2)}) copy-start(bf16[1024,1024]{1,0:T(8,128)(2,1)} %param.17) | copy-start | bytes 6291460
  6.5 148.5 %all-gather.5.cloned.1.call-start = ((), (), s32[]{:S(2)}) async-start(), calls=%async_computation | async-start | bytes 17301504 | tf_op jit(solution)/shard_map/all_gather | solution.py:44
  8.9 4.0 %copy-start.6 = (s32[128]{0:T(128)S(1)}, s32[128]{0:T(128)}, u32[]{:S(2)}) copy-start(s32[128]{0:T(128)} %param.14) | copy-start | bytes 1540
  9.0 50.1 %copy-start.1 = (bf16[128,1024]{1,0:T(8,128)(2,1)S(1)}, bf16[128,1024]{1,0:T(8,128)(2,1)}, u32[]{:S(2)}) copy-start(bf16[128,1024]{1,0:T(8,128)(2,1)} %param.12) | copy-start | bytes 786436
  9.0 50.1 %copy-start.5 = (f32[1024]{0:T(1024)S(1)}, f32[1024]{0:T(1024)}, u32[]{:S(2)}) copy-start(f32[1024]{0:T(1024)} %param.15) | copy-start | bytes 12292
  12.9 311.6 %all-gather.7.cloned.1.call-start = ((), (), s32[]{:S(2)}) async-start(), calls=%async_computation.1 | async-start | bytes 4325376 | tf_op jit(solution)/shard_map/all_gather | solution.py:67
  59.1 2.3 copy-start.7
  332.0 8.0 %copy-start.2 = (bf16[5,512,512]{2,1,0:T(8,128)(2,1)S(1)}, bf16[5,512,512]{2,1,0:T(8,128)(2,1)}, u32[]{:S(2)}) copy-start(bf16[5,512,512]{2,1,0:T(8,128)(2,1)} %param.19) | copy-start | bytes 7864324
  332.2 9.4 %collective-permute-start.1 = (bf16[2,512]{0,1:T(8,128)(2,1)S(1)}, bf16[2,512]{0,1:T(8,128)(2,1)S(1)}, u32[]{:S(2)}, u32[]{:S(2)}) collective-permute-start(bf16[2,512]{0,1:T(8,128)(2,1)S(1)} %get-tuple-element.107), channel_id=1, source_target_pairs={{8,0},{16,8},{24,16},{32,24},{40,32},{48,40},{56,48},{64,56},{72,6... | collective-permute-start | bytes 6152 | tf_op jit(solution)/shard_map/ppermute | solution.py:19
  334.7 5.3 %collective-permute-start = (bf16[2,512]{0,1:T(8,128)(2,1)S(1)}, bf16[2,512]{0,1:T(8,128)(2,1)S(1)}, u32[]{:S(2)}, u32[]{:S(2)}) collective-permute-start(bf16[2,512]{0,1:T(8,128)(2,1)S(1)} %get-tuple-element.106), channel_id=1, source_target_pairs={{0,8},{8,16},{16,24},{24,32},{32,40},{40,48},{48,56},{56,64},{64,7... | collective-permute-start | bytes 6152 | tf_op jit(solution)/shard_map/ppermute | solution.py:18
  341.6 0.8 copy-start.3
  342.4 1.3 copy-start.4
Sparse Core Ops, SparseCore 0:
  13.0 141.9 all-gather.4
  240.9 83.4 all-gather.6
where the time goes:
time: 360 us; the launch traced here: 354 us
  local copies, waits for them, and re-layouts  103 us (29%)
  blocking collectives  82.5 us (23%)
  waiting for transfers between devices  80.8 us (22%)
  matrix products  46.3 us (13%)
  other arithmetic  21.2 us (6%)
  between operations  13.7 us (4%)
  starting transfers between devices  5.92 us (2%)
    gather x13, local copies, waits for them, and re-layouts, local(): unit_of = jnp.searchsorted(ends, frame_pos, side='right')  58 us
    all_gather x1, waiting for transfers between devices, local(): kv_rows = lax.all_gather(kv_local, 'seq', axis=0, tiled=True)  56.1 us
    all_gather x1, blocking collectives, local(): lax.all_gather(seg_wire, 'seq', axis=0, tiled=True).astype(jnp.float32)  46 us
    all_gather x1, blocking collectives, local(): lax.all_gather(durations.astype(jnp.bfloat16), 'seq', axis=0, tiled=True)  36.5 us
    all_gather x1, waiting for transfers between devices, local(): lax.all_gather(reduced, 'seq', axis=0, tiled=True)  24.3 us
    slice x2, local copies, waits for them, and re-layouts, local(): keys = kv_rows[:, :width].reshape(count, HEADS, head_size)  23.3 us
    dot_general x1, matrix products, local(): jnp.einsum('hqk,khd->hqd', expo.astype(jnp.bfloat16), values, preferred_e...  16.8 us
    reduce_sum x1, other arithmetic, local(): total = jnp.sum(expo, axis=2)  15.9 us
  transfers between devices with their start and end apart: 4, of which 3 were waited for; matrix products, arithmetic and copies ran while one was open for 18% of the time, Pallas kernels for 0%

commit v1 on v0

v1 whole, which is shorter than its diff:
```python
import functools

import jax
import jax.numpy as jnp
from jax import lax
from jax.experimental import pallas as pl
from jax.experimental.pallas import tpu as pltpu
from jax.sharding import PartitionSpec as P

MESH = pl.DeviceIdType.MESH
SEQ = 32
CHIPS = 16
HEADS = 16
HEAD = 64
ROWS = 128
WIDTH = 1024
UNITS = 4096
CHANNELS = 512
KERNEL = 5
FRAMES = 768
STEP = 96
STEPS = FRAMES // STEP
KEYS = 512
NEG = -1e30
VMEM_LIMIT = 60 * 1024 * 1024


def seq(index):
    return {"seq": index}


def greet_all(me):
    barrier = pltpu.get_barrier_semaphore()

    def greet(i, carry):
        pl.semaphore_signal(
            barrier, 1, device_id=seq(lax.rem(me + i, SEQ)), device_id_type=MESH
        )
        return carry

    lax.fori_loop(1, SEQ, greet, 0)


def await_all():
    pl.semaphore_wait(pltpu.get_barrier_semaphore(), SEQ - 1)


def group_at(own, i):
    flip = own + 1 - 2 * lax.rem(own, 2)
    if i == 0:
        return flip
    if i == 1:
        return lax.rem(flip + 2, 4)
    if i == 2:
        return lax.rem(own + 2, 4)
    return own


def low_lanes(rows):
    return lax.broadcasted_iota(jnp.int32, (rows, 128), 1) < HEAD


def spread_kernel(
    units_ref,
    gain_ref,
    meta_ref,
    w_ref,
    kv_ref,
    q_ref,
    seg_ref,
    start_ref,
    end_ref,
    range_ref,
    h_ref,
    wbuf,
    send_kv,
    send_q,
    meta_all,
    w_sem,
    kv_send,
    kv_recv,
    q_send,
    q_recv,
    pass_send,
    pass_recv,
    meta_send,
    meta_recv,
    own_sem,
):
    me = lax.axis_index("seq")
    core = lax.rem(me, 2)
    chip = me // 2
    sibling = me + 1 - 2 * core
    own = chip // 4
    greet_all(me)

    def w_copy(i, t):
        g = group_at(own, i)
        return pltpu.make_async_copy(
            w_ref.at[:, pl.ds(t * WIDTH + g * 256, 256)], wbuf.at[i, t], w_sem.at[i, t]
        )

    for i in range(4):
        for t in range(3):
            w_copy(i, t).start()

    x = units_ref[...].astype(jnp.float32)
    mean = jnp.mean(x, axis=-1, keepdims=True)
    centred = x - mean
    variance = jnp.mean(centred * centred, axis=-1, keepdims=True)
    h_ref[...] = (centred / jnp.sqrt(variance + 1e-05) * gain_ref[...]).astype(jnp.bfloat16)

    await_all()

    def meta_copy(i, source):
        return pltpu.make_async_remote_copy(
            src_ref=meta_ref,
            dst_ref=meta_all.at[source],
            send_sem=meta_send.at[i],
            recv_sem=meta_recv.at[source],
            device_id=seq(lax.rem(me + i, SEQ)),
            device_id_type=MESH,
        )

    def send_meta(i, carry):
        meta_copy(i, me).start()
        return carry

    lax.fori_loop(1, SEQ, send_meta, 0)
    own_meta = pltpu.make_async_copy(meta_ref, meta_all.at[me], own_sem.at[2])
    own_meta.start()

    def kv_copy(head, source):
        return pltpu.make_async_remote_copy(
            src_ref=send_kv.at[head],
            dst_ref=kv_ref.at[2 * source + core],
            send_sem=kv_send.at[head],
            recv_sem=kv_recv.at[source],
            device_id=seq(2 * head + core),
            device_id_type=MESH,
        )

    def q_copy(head, source):
        return pltpu.make_async_remote_copy(
            src_ref=send_q.at[head],
            dst_ref=q_ref.at[source],
            send_sem=q_send.at[head],
            recv_sem=q_recv.at[source],
            device_id=seq(2 * head + core),
            device_id_type=MESH,
        )

    own_kv = pltpu.make_async_copy(send_kv.at[chip], kv_ref.at[me], own_sem.at[0])
    own_q = pltpu.make_async_copy(send_q.at[chip], q_ref.at[chip], own_sem.at[1])
    own_pass = pltpu.make_async_remote_copy(
        src_ref=send_kv.at[chip],
        dst_ref=kv_ref.at[me],
        send_sem=pass_send.at[chip],
        recv_sem=pass_recv.at[chip],
        device_id=seq(sibling),
        device_id_type=MESH,
    )

    low = low_lanes(ROWS)
    low_half = low_lanes(ROWS // 2)
    for i in range(4):
        g = group_at(own, i)
        for t in range(3):
            w_copy(i, t).wait()
        h = h_ref[...]
        q4, k4, v4 = (
            jnp.dot(h, wbuf[i, t], preferred_element_type=jnp.float32) for t in range(3)
        )
        for j in range(2):
            at = slice(128 * j, 128 * j + 128)
            q2, k2, v2 = q4[:, at] * 0.125, k4[:, at], v4[:, at]
            v_turned, k_turned = pltpu.roll(v2, HEAD, 1), pltpu.roll(k2, HEAD, 1)
            q_turned = pltpu.roll(q2, HEAD, 1)
            first = 4 * g + 2 * j
            send_kv[first] = jnp.where(low, k2, v_turned).astype(jnp.bfloat16)
            send_kv[first + 1] = jnp.where(low, k_turned, v2).astype(jnp.bfloat16)
            send_q[first] = jnp.where(low_half, q2[:64], q_turned[64:]).astype(jnp.bfloat16)
            send_q[first + 1] = jnp.where(low_half, q_turned[:64], q2[64:]).astype(jnp.bfloat16)
        for r in range(4):
            head = 4 * g + lax.rem(chip + r, 4)
            if i < 3:
                kv_copy(head, chip).start()
                q_copy(head, chip).start()
            elif r == 0:
                own_kv.start()
                own_pass.start()
                own_q.start()
            else:
                kv_copy(head, chip).start()
                q_copy(head, chip).start()

    def await_meta(i, carry):
        meta_copy(i, lax.rem(me + SEQ - i, SEQ)).wait()
        return carry

    lax.fori_loop(1, SEQ, await_meta, 0)
    own_meta.wait()

    seg = meta_all[:, 0, :]
    dur = meta_all[:, 1, :].astype(jnp.float32)
    lower = (
        lax.broadcasted_iota(jnp.int32, (128, 128), 0)
        <= lax.broadcasted_iota(jnp.int32, (128, 128), 1)
    ).astype(jnp.float32).astype(jnp.bfloat16)
    earlier = (
        lax.broadcasted_iota(jnp.int32, (SEQ, SEQ), 0)
        > lax.broadcasted_iota(jnp.int32, (SEQ, SEQ), 1)
    ).astype(jnp.float32).astype(jnp.bfloat16)
    dur16 = dur.astype(jnp.bfloat16)
    within = jnp.dot(dur16, lower, preferred_element_type=jnp.float32)
    before = jnp.dot(earlier, dur16, preferred_element_type=jnp.float32)
    ends = within + jnp.sum(before, axis=1, keepdims=True)
    seg_ref[...] = seg
    start_ref[...] = (ends - dur).astype(jnp.int32)
    end_ref[...] = ends.astype(jnp.int32)

    first_seg, last_seg = seg[:, 0:1], seg[:, 127:128]
    lane = lax.broadcasted_iota(jnp.int32, (SEQ, 128), 1)
    lo = jnp.zeros((SEQ, 1), jnp.int32)
    hi = jnp.zeros((SEQ, 1), jnp.int32)
    for s in range(8):
        below = jnp.sum((seg < s).astype(jnp.float32)).astype(jnp.int32)
        upto = jnp.sum((seg <= s).astype(jnp.float32)).astype(jnp.int32)
        lo = jnp.where(first_seg == s, below, lo)
        hi = jnp.where(last_seg == s, upto, hi)
    range_ref[0:SEQ, :] = jnp.where(lane == 0, lo, jnp.where(lane == 1, hi, 0))
    lane8 = lax.broadcasted_iota(jnp.int32, (8, 128), 1)
    block = jnp.zeros((8, 128), jnp.int32)
    for f in range(STEPS):
        t0 = (FRAMES * me + STEP * f - KERNEL // 2).astype(jnp.float32)
        passed = jnp.sum((ends <= t0).astype(jnp.float32)).astype(jnp.int32)
        block = jnp.where(lane8 == f, passed, block)
    range_ref[SEQ:, :] = block

    def passing(source):
        return pltpu.make_async_remote_copy(
            src_ref=kv_ref.at[2 * source + core],
            dst_ref=kv_ref.at[2 * source + core],
            send_sem=pass_send.at[source],
            recv_sem=pass_recv.at[source],
            device_id=seq(sibling),
            device_id_type=MESH,
        )

    for i in range(4):
        for r in range(4):
            if i == 3 and r == 0:
                continue
            source = 4 * group_at(own, i) + lax.rem(chip + 4 - r, 4)
            kv_copy(source, source).wait_recv()
            passing(source).start()

    for i in range(4):
        for r in range(4):
            source = 4 * group_at(own, i) + lax.rem(chip + 4 - r, 4)
            if i == 3 and r == 0:
                own_kv.wait()
                own_q.wait()
                own_pass.wait()
            else:
                q_copy(source, source).wait()
                kv_copy(source, source).wait_send()
                passing(source).wait()


def spread(units, gain, meta, w_qkv):
    any_space = pl.BlockSpec(memory_space=pl.ANY)
    vmem = pl.BlockSpec(memory_space=pltpu.VMEM)
    dma = pltpu.SemaphoreType.DMA
    return pl.pallas_call(
        spread_kernel,
        out_shape=(
            jax.ShapeDtypeStruct((SEQ, ROWS, 128), jnp.bfloat16),
            jax.ShapeDtypeStruct((CHIPS, ROWS // 2, 128), jnp.bfloat16),
            jax.ShapeDtypeStruct((SEQ, 128), jnp.int32),
            jax.ShapeDtypeStruct((SEQ, 128), jnp.int32),
            jax.ShapeDtypeStruct((SEQ, 128), jnp.int32),
            jax.ShapeDtypeStruct((SEQ + 8, 128), jnp.int32),
        ),
        in_specs=[vmem, vmem, vmem, any_space],
        out_specs=(any_space, any_space, vmem, vmem, vmem, vmem),
        scratch_shapes=[
            pltpu.VMEM((ROWS, WIDTH), jnp.bfloat16),
            pltpu.VMEM((4, 3, WIDTH, 256), jnp.bfloat16),
            pltpu.VMEM((HEADS, ROWS, 128), jnp.bfloat16),
            pltpu.VMEM((HEADS, ROWS // 2, 128), jnp.bfloat16),
            pltpu.VMEM((SEQ, 2, 128), jnp.int32),
            dma((4, 3)),
            dma((HEADS,)),
            dma((HEADS,)),
            dma((HEADS,)),
            dma((HEADS,)),
            dma((HEADS,)),
            dma((HEADS,)),
            dma((SEQ,)),
            dma((SEQ,)),
            dma((3,)),
        ],
        compiler_params=pltpu.CompilerParams(
            collective_id=1, has_side_effects=True, vmem_limit_bytes=VMEM_LIMIT
        ),
        name="spread",
    )(units, gain, meta, w_qkv)


def attend_kernel(range_ref, kv_ref, q_ref, seg_ref, out_ref, v1_ref, s_ref, qs_ref):
    core = lax.rem(lax.axis_index("seq"), 2)
    low = low_lanes(KEYS)

    def prepare(i, carry):
        at = pl.ds(pl.multiple_of(i * KEYS, KEYS), KEYS)
        v1_ref[at, :] = jnp.where(low, 1.0, kv_ref[at, :].astype(jnp.float32)).astype(
            jnp.bfloat16
        )
        return carry

    lax.fori_loop(0, UNITS // KEYS, prepare, 0)
    low_half = low_lanes(ROWS // 2)

    def pair(p, carry):
        rows = []
        for e in range(2):
            packed = q_ref[2 * p + e].astype(jnp.float32)
            rows.append(jnp.where(low_half, packed, 0.0))
            rows.append(jnp.where(low_half, pltpu.roll(packed, HEAD, 1), 0.0))
            seg_row = seg_ref[pl.ds(4 * p + 2 * e + core, 1), :].astype(jnp.float32)
            qs_ref[128 * e : 128 * e + 128, :] = jnp.transpose(
                jnp.broadcast_to(seg_row, (128, 128))
            )
        q = jnp.concatenate(rows, axis=0).astype(jnp.bfloat16)
        first = 4 * p + core
        lo, hi = range_ref[first, 0], range_ref[first + 2, 1]
        lo = lo // 128
        steps = (hi - 128 * lo + KEYS - 1) // KEYS
        base = jnp.minimum(lo, SEQ - (KEYS // 128) * steps)

        def score(i, top):
            block = base + (KEYS // 128) * i
            at = pl.ds(pl.multiple_of(block * 128, 128), KEYS)
            s = lax.dot_general(
                q, kv_ref[at, :], (((1,), (1,)), ((), ())), preferred_element_type=jnp.float32
            )
            for t in range(KEYS // 128):
                seg_row = seg_ref[pl.ds(block + t, 1), :].astype(jnp.float32)
                masked = jnp.where(qs_ref[...] == seg_row, s[:, 128 * t : 128 * t + 128], NEG)
                s_ref[i, :, 128 * t : 128 * t + 128] = masked
                top = jnp.maximum(top, masked)
            return top

        top = lax.fori_loop(0, steps, score, jnp.full((256, 128), NEG, jnp.float32))
        top = jnp.max(top, axis=1, keepdims=True)

        def gather(i, acc):
            at = pl.ds(pl.multiple_of((base + (KEYS // 128) * i) * 128, 128), KEYS)
            weights = jnp.exp(s_ref[i] - top).astype(jnp.bfloat16)
            return acc + jnp.dot(weights, v1_ref[at, :], preferred_element_type=jnp.float32)

        acc = lax.fori_loop(0, steps, gather, jnp.zeros((256, 128), jnp.float32))
        out = acc / pltpu.roll(acc, HEAD, 1)
        for e in range(2):
            upper, under = out[128 * e : 128 * e + 64], out[128 * e + 64 : 128 * e + 128]
            out_ref[2 * p + e] = jnp.where(low_half, pltpu.roll(upper, HEAD, 1), under).astype(
                jnp.bfloat16
            )
        return carry

    lax.fori_loop(0, CHIPS // 2, pair, 0)


def attend(ranges, kv, q, seg):
    vmem = pl.BlockSpec(memory_space=pltpu.VMEM)
    return pl.pallas_call(
        attend_kernel,
        out_shape=jax.ShapeDtypeStruct((CHIPS, ROWS // 2, 128), jnp.bfloat16),
        in_specs=[pl.BlockSpec(memory_space=pltpu.SMEM), vmem, vmem, vmem],
        out_specs=vmem,
        scratch_shapes=[
            pltpu.VMEM((UNITS, 128), jnp.bfloat16),
            pltpu.VMEM((UNITS // KEYS, 256, KEYS), jnp.float32),
            pltpu.VMEM((256, 128), jnp.float32),
        ],
        compiler_params=pltpu.CompilerParams(vmem_limit_bytes=VMEM_LIMIT),
        name="attend",
    )(ranges, kv.reshape(UNITS, 128), q, seg)


def mix_kernel(
    o_ref, units_ref, w_out_ref, w_proj_ref, out_ref, landed, attended, o_send, o_recv, own_sem
):
    me = lax.axis_index("seq")
    core = lax.rem(me, 2)
    chip = me // 2
    greet_all(me)
    await_all()

    def o_copy(target, source):
        return pltpu.make_async_remote_copy(
            src_ref=o_ref.at[target],
            dst_ref=landed.at[source],
            send_sem=o_send.at[target],
            recv_sem=o_recv.at[source],
            device_id=seq(2 * target + core),
            device_id_type=MESH,
        )

    def send(i, carry):
        o_copy(lax.rem(chip + i, CHIPS), chip).start()
        return carry

    lax.fori_loop(1, CHIPS, send, 0)
    own = pltpu.make_async_copy(o_ref.at[chip], landed.at[chip], own_sem)
    own.start()

    def receive(i, carry):
        source = lax.rem(chip + CHIPS - i, CHIPS)
        o_copy(source, source).wait()
        return carry

    lax.fori_loop(1, CHIPS, receive, 0)
    own.wait()

    low_half = low_lanes(ROWS // 2)
    for j in range(HEADS // 2):
        a, b = landed[2 * j].astype(jnp.float32), landed[2 * j + 1].astype(jnp.float32)
        upper = jnp.where(low_half, a, pltpu.roll(b, HEAD, 1))
        under = jnp.where(low_half, pltpu.roll(a, HEAD, 1), b)
        attended[:64, 128 * j : 128 * j + 128] = upper.astype(jnp.bfloat16)
        attended[64:, 128 * j : 128 * j + 128] = under.astype(jnp.bfloat16)
    mixed = jnp.dot(attended[...], w_out_ref[...], preferred_element_type=jnp.float32)
    mixed = (mixed + units_ref[...].astype(jnp.float32)).astype(jnp.bfloat16)
    out_ref[...] = jnp.dot(mixed, w_proj_ref[...], preferred_element_type=jnp.float32).astype(
        jnp.bfloat16
    )


def mix(o, units, w_out, w_proj):
    vmem = pl.BlockSpec(memory_space=pltpu.VMEM)
    dma = pltpu.SemaphoreType.DMA
    return pl.pallas_call(
        mix_kernel,
        out_shape=jax.ShapeDtypeStruct((ROWS, CHANNELS), jnp.bfloat16),
        in_specs=[vmem] * 4,
        out_specs=vmem,
        scratch_shapes=[
            pltpu.VMEM((HEADS, ROWS // 2, 128), jnp.bfloat16),
            pltpu.VMEM((ROWS, WIDTH), jnp.bfloat16),
            dma((CHIPS,)),
            dma((CHIPS,)),
            dma,
        ],
        compiler_params=pltpu.CompilerParams(
            collective_id=2, has_side_effects=True, vmem_limit_bytes=VMEM_LIMIT
        ),
        name="mix",
    )(o, units, w_out, w_proj)


def frames_kernel(
    range_ref, reduced_ref, start_ref, end_ref, w_ref, b_ref, gain_ref, out_ref, stacked
):
    me = lax.axis_index("seq")
    bias, gain = b_ref[...], gain_ref[...]

    def step(f, carry):
        block = jnp.minimum(range_ref[SEQ, f] // 128, SEQ - 2)
        starts = jnp.concatenate(
            [start_ref[pl.ds(block, 1), :], start_ref[pl.ds(block + 1, 1), :]], axis=1
        )
        ends = jnp.concatenate(
            [end_ref[pl.ds(block, 1), :], end_ref[pl.ds(block + 1, 1), :]], axis=1
        )
        window = reduced_ref[pl.ds(pl.multiple_of(block * 128, 128), 256), :]
        frame = (
            lax.broadcasted_iota(jnp.int32, (STEP, 256), 0)
            + FRAMES * me
            + STEP * f
            - KERNEL // 2
        )
        centre = None
        for j in range(KERNEL):
            chosen = jnp.where((frame + j >= starts) & (frame + j < ends), 1.0, 0.0)
            rows = jnp.dot(
                chosen.astype(jnp.bfloat16), window, preferred_element_type=jnp.float32
            )
            if j == KERNEL // 2:
                centre = rows
            stacked[:, CHANNELS * j : CHANNELS * j + CHANNELS] = rows.astype(jnp.bfloat16)
        conv = jnp.dot(stacked[...], w_ref[...], preferred_element_type=jnp.float32) + bias
        value = jnp.maximum(conv, 0.0)
        mean = jnp.mean(value, axis=-1, keepdims=True)
        centred = value - mean
        variance = jnp.mean(centred * centred, axis=-1, keepdims=True)
        result = centre + centred / jnp.sqrt(variance + 1e-05) * gain
        out_ref[pl.ds(pl.multiple_of(f * STEP, STEP), STEP), :] = result.astype(jnp.bfloat16)
        return carry

    lax.fori_loop(0, STEPS, step, 0)


def frames(ranges, reduced, starts, ends, conv_w, conv_b, conv_gain):
    vmem = pl.BlockSpec(memory_space=pltpu.VMEM)
    return pl.pallas_call(
        frames_kernel,
        out_shape=jax.ShapeDtypeStruct((FRAMES, CHANNELS), jnp.bfloat16),
        in_specs=[pl.BlockSpec(memory_space=pltpu.SMEM)] + [vmem] * 6,
        out_specs=vmem,
        scratch_shapes=[pltpu.VMEM((STEP, KERNEL * CHANNELS), jnp.bfloat16)],
        compiler_params=pltpu.CompilerParams(vmem_limit_bytes=VMEM_LIMIT),
        name="frames",
    )(ranges, reduced, starts, ends, conv_w, conv_b, conv_gain)


def local(units, durations, seg_ids, ln_gain, w_qkv, w_out, w_proj, conv_w, conv_b, conv_gain):
    meta = jnp.stack([seg_ids, durations])
    kv, q, seg, starts, ends, ranges = spread(units, ln_gain.reshape(1, WIDTH), meta, w_qkv)
    o = attend(ranges, kv, q, seg)
    reduced = mix(o, units, w_out, w_proj)
    whole = lax.all_gather(reduced, "seq", axis=0, tiled=True)
    return frames(
        ranges,
        whole,
        starts,
        ends,
        conv_w.reshape(KERNEL * CHANNELS, CHANNELS),
        conv_b.reshape(1, CHANNELS),
        conv_gain.reshape(1, CHANNELS),
    )


def solution(mesh):
    parted = P(("grp", "seq"))
    wide = P(("grp", "seq"), None)
    return jax.shard_map(
        local,
        mesh=mesh,
        in_specs=(wide, parted, parted) + (P(),) * 7,
        out_specs=wide,
        check_vma=False,
    )
```

time: 360 us -> 188 us (0.52); the launches traced: 354 us -> 188 us
  local copies, waits for them, and re-layouts: 103 us -> 0 us
  Pallas kernels: 0 us -> 85.9 us
  blocking collectives: 82.5 us -> 0 us
  matrix products: 46.3 us -> 0 us
  other arithmetic: 21.2 us -> 1.24 us
  waiting for transfers between devices: 80.8 us -> 87.1 us
  starting transfers between devices: 5.92 us -> 0.01 us
    pallas_call x0 -> x4, Pallas kernels: none -> 85.9 us  [the longest x1 35.3 us: spread(): pl.pallas_call(spread_kernel, out_shape=(jax.ShapeDtypeStruct((SEQ, ROWS,...]
    all_gather x2 -> x0, blocking collectives: 82.5 us -> none  [the longest x1 46 us: local(): lax.all_gather(seg_wire, 'seq', axis=0, tiled=True).astype(jnp.float32)]
    gather x15 -> x0, local copies, waits for them, and re-layouts: 65.5 us -> none  [the longest x13 58 us: local(): unit_of = jnp.searchsorted(ends, frame_pos, side='right')]
    dot_general x10 -> x0, matrix products: 46.3 us -> none  [the longest x1 16.8 us: local(): jnp.einsum('hqk,khd->hqd', expo.astype(jnp.bfloat16), values, preferred_e...]
    slice x5 -> x0, local copies, waits for them, and re-layouts: 34.8 us -> none  [the longest x2 23.3 us: local(): keys = kv_rows[:, :width].reshape(count, HEADS, head_size)]
    reduce_sum x4 -> x0, other arithmetic: 18.5 us -> none  [the longest x1 15.9 us: local(): total = jnp.sum(expo, axis=2)]
    all_gather x2 -> x1, waiting for transfers between devices: 80.5 us -> 87.1 us  [local(): whole = lax.all_gather(reduced, 'seq', axis=0, tiled=True)]
    ppermute x2 -> x0, starting transfers between devices: 5.87 us -> none  [the longest x1 3.4 us: extended(): before = lax.ppermute(last, axis, up)]
  transfers between devices with their start and end apart: 4 -> 1, of which waited for: 3 -> 1; matrix products, arithmetic and copies ran while one was open for 18% -> 0% of each run, Pallas kernels for 0% -> 0%
where the time goes in v1:
time: 188 us
  waiting for transfers between devices  87.1 us (46%)
  Pallas kernels  85.9 us (46%)
  between operations  13.4 us (7%)
    all_gather x1, waiting for transfers between devices, local(): whole = lax.all_gather(reduced, 'seq', axis=0, tiled=True)  87.1 us
    pallas_call x1, Pallas kernels, spread(): pl.pallas_call(spread_kernel, out_shape=(jax.ShapeDtypeStruct((SEQ, ROWS,...  35.3 us
    pallas_call x1, Pallas kernels, attend(): pl.pallas_call(attend_kernel, out_shape=jax.ShapeDtypeStruct((CHIPS, ROWS...  21.1 us
    pallas_call x1, Pallas kernels, mix(): pl.pallas_call(mix_kernel, out_shape=jax.ShapeDtypeStruct((ROWS, CHANNELS...  17.7 us
    pallas_call x1, Pallas kernels, frames(): pl.pallas_call(frames_kernel, out_shape=jax.ShapeDtypeStruct((FRAMES, CHA...  11.7 us
  transfers between devices with their start and end apart: 1, of which 1 were waited for; matrix products, arithmetic and copies ran while one was open for 0% of the time, Pallas kernels for 0%

profile of v1, /device:TPU:1, one launch (start us, length us, event | category | flops | bytes accessed | tf_op | source)
XLA Modules:
  0.0 187.6 jit_solution(3821563352994824839)
XLA Ops:
  6.5 0.0 all-gather.2.cloned.1.call-start
  6.5 1.2 pad_add_fusion.meta_ref
  7.8 35.3 %spread.1 = (bf16[32,128,128]{2,1,0:T(8,128)(2,1)}, bf16[16,64,128]{2,1,0:T(8,128)(2,1)}, s32[32,128]{1,0:T(8,128)}, s32[32,128]{1,0:T(8,128)}, s32[32,128]{1,0:T(8,128)}, /*index=5*/s32[40,128]{1,0:T(8,128)}) custom-call(bf16[128,1024]{1,0:T(8,128)(2,1)} %units_ref.3, f32[1,1024]{1,0:T(1,128)} %bitcast.9, s32[2,128]{1,0:T(2,128)} %pad_add_fusion.meta_ref, ...), custom_call_target="tpu_custom_call" | custom-call | tf_op jit(solution)/shard_map/spread/pallas_call | solution.py:275
  43.1 21.1 %attend.1.o_ref = bf16[16,64,128]{2,1,0:T(8,128)(2,1)} custom-call(s32[40,128]{1,0:T(8,128)} %get-tuple-element.11.range_ref, bf16[4096,128]{1,0:T(8,128)(2,1)} %bitcast.8, bf16[16,64,128]{2,1,0:T(8,128)(2,1)} %get-tuple-element.13.q_ref, s32[32,128]{1,0:T(8,128)} %get-tuple-element.14.seg_ref), custom_call_target="tpu_custom_call" | custom-call | tf_op jit(solution)/shard_map/attend/pallas_call | solution.py:377
  64.2 17.7 %mix.1 = bf16[128,512]{1,0:T(8,128)(2,1)} custom-call(bf16[16,64,128]{2,1,0:T(8,128)(2,1)} %attend.1.o_ref, bf16[128,1024]{1,0:T(8,128)(2,1)} %units_ref.3, bf16[1024,1024]{1,0:T(8,128)(2,1)} %w_out_ref.1, bf16[1024,512]{1,0:T(8,128)(2,1)} %w_proj_ref.1), custom_call_target="tpu_custom_call" | custom-call | tf_op jit(solution)/shard_map/mix/pallas_call | solution.py:444
  82.0 0.0 all-gather.2.cloned.1.call-update
  82.0 87.1 %all-gather.2.cloned.1.call-done.reduced_ref = bf16[4096,512]{1,0:T(8,128)(2,1)} async-done(((bf16[128,512]{1,0:T(8,128)(2,1)}), bf16[4096,512]{1,0:T(8,128)(2,1)}) %all-gather.2.cloned.1.call-update) | async-done | bytes 4194320 | tf_op jit(solution)/shard_map/all_gather | solution.py:523
  169.1 11.7 %frames.1 = bf16[768,512]{1,0:T(8,128)(2,1)} custom-call(s32[40,128]{1,0:T(8,128)} %get-tuple-element.11.range_ref, bf16[4096,512]{1,0:T(8,128)(2,1)} %all-gather.2.cloned.1.call-done.reduced_ref, s32[32,128]{1,0:T(8,128)} %get-tuple-element.15.start_ref, s32[32,128]{1,0:T(8,128)} %get-tuple-element.16.end_ref, bf16[2560,512]{1,0:T(8,128)(2,1)} %bitcast.7, ...), custom_call_target="tpu_custom_call" | custom-call | tf_op jit(solution)/shard_map/frames/pallas_call | solution.py:507
Async XLA Ops:
  6.5 162.5 %all-gather.2.cloned.1.call-start = ((), (), s32[]{:S(2)}) async-start(), calls=%async_computation | async-start | bytes 4325376 | tf_op jit(solution)/shard_map/all_gather | solution.py:523
Sparse Core Ops, SparseCore 0:
  82.1 86.9 all-gather.1

commit v2 on v1

v2 whole, which is shorter than its diff:
```python
import functools

import jax
import jax.numpy as jnp
from jax import lax
from jax.experimental import pallas as pl
from jax.experimental.pallas import tpu as pltpu
from jax.sharding import PartitionSpec as P

MESH = pl.DeviceIdType.MESH
SEQ = 32
CHIPS = 16
HEADS = 16
HEAD = 64
ROWS = 128
WIDTH = 1024
UNITS = 4096
CHANNELS = 512
KERNEL = 5
FRAMES = 768
STEP = 96
STEPS = FRAMES // STEP
TILE = 256
BLOCKS = 8
GROUPS = 8
NEG = -1e30
MIB = 1024 * 1024
META = SEQ + 16


def seq(index):
    return {"seq": index}


def greet_all(me):
    barrier = pltpu.get_barrier_semaphore()

    def greet(i, carry):
        pl.semaphore_signal(
            barrier, 1, device_id=seq(lax.rem(me + i, SEQ)), device_id_type=MESH
        )
        return carry

    lax.fori_loop(1, SEQ, greet, 0)


def await_all(more=0):
    pl.semaphore_wait(pltpu.get_barrier_semaphore(), SEQ - 1 + more)


def group_at(own, i):
    flip = own + 1 - 2 * lax.rem(own, 2)
    if i == 0:
        return flip
    if i == 1:
        return lax.rem(flip + 2, 4)
    if i == 2:
        return lax.rem(own + 2, 4)
    return own


def low_lanes(rows):
    return lax.broadcasted_iota(jnp.int32, (rows, 128), 1) < HEAD


def spread_kernel(
    units_ref,
    gain_ref,
    meta_ref,
    w_ref,
    kv_ref,
    q_ref,
    mark_ref,
    seg_ref,
    start_ref,
    end_ref,
    range_ref,
    h_ref,
    wbuf,
    send_kv,
    send_q,
    meta_all,
    flags,
    w_sem,
    kv_send,
    kv_recv,
    q_send,
    q_recv,
    pass_send,
    pass_recv,
    meta_send,
    meta_recv,
    flag_send,
    flag_recv,
    own_sem,
):
    me = lax.axis_index("seq")
    part = lax.axis_index("grp")
    core = lax.rem(me, 2)
    chip = me // 2
    sibling = me + 1 - 2 * core
    own = chip // 4
    greet_all(me)

    def greet_part(i, carry):
        pl.semaphore_signal(
            pltpu.get_barrier_semaphore(),
            1,
            device_id={"grp": lax.rem(part + i, GROUPS)},
            device_id_type=MESH,
        )
        return carry

    lax.fori_loop(1, GROUPS, greet_part, 0)

    def w_copy(i, t):
        g = group_at(own, i)
        return pltpu.make_async_copy(
            w_ref.at[:, pl.ds(t * WIDTH + g * 256, 256)], wbuf.at[i, t], w_sem.at[i, t]
        )

    for i in range(4):
        for t in range(3):
            w_copy(i, t).start()

    x = units_ref[...].astype(jnp.float32)
    mean = jnp.mean(x, axis=-1, keepdims=True)
    centred = x - mean
    variance = jnp.mean(centred * centred, axis=-1, keepdims=True)
    h_ref[...] = (centred / jnp.sqrt(variance + 1e-05) * gain_ref[...]).astype(jnp.bfloat16)

    await_all(GROUPS - 1)

    def meta_copy(i, source):
        return pltpu.make_async_remote_copy(
            src_ref=meta_ref,
            dst_ref=meta_all.at[source],
            send_sem=meta_send.at[i],
            recv_sem=meta_recv.at[source],
            device_id=seq(lax.rem(me + i, SEQ)),
            device_id_type=MESH,
        )

    def send_meta(i, carry):
        meta_copy(i, me).start()
        return carry

    lax.fori_loop(1, SEQ, send_meta, 0)
    own_meta = pltpu.make_async_copy(meta_ref, meta_all.at[me], own_sem.at[2])
    own_meta.start()

    def kv_copy(head, source):
        return pltpu.make_async_remote_copy(
            src_ref=send_kv.at[head],
            dst_ref=kv_ref.at[2 * source + core],
            send_sem=kv_send.at[head],
            recv_sem=kv_recv.at[source],
            device_id=seq(2 * head + core),
            device_id_type=MESH,
        )

    def q_copy(head, source):
        return pltpu.make_async_remote_copy(
            src_ref=send_q.at[head],
            dst_ref=q_ref.at[source],
            send_sem=q_send.at[head],
            recv_sem=q_recv.at[source],
            device_id=seq(2 * head + core),
            device_id_type=MESH,
        )

    own_kv = pltpu.make_async_copy(send_kv.at[chip], kv_ref.at[me], own_sem.at[0])
    own_q = pltpu.make_async_copy(send_q.at[chip], q_ref.at[chip], own_sem.at[1])
    own_pass = pltpu.make_async_remote_copy(
        src_ref=send_kv.at[chip],
        dst_ref=kv_ref.at[me],
        send_sem=pass_send.at[chip],
        recv_sem=pass_recv.at[chip],
        device_id=seq(sibling),
        device_id_type=MESH,
    )

    low = low_lanes(ROWS // 2)
    for i in range(4):
        g = group_at(own, i)
        for t in range(3):
            w_copy(i, t).wait()
        h = h_ref[...]
        q4, k4, v4 = (
            jnp.dot(h, wbuf[i, t], preferred_element_type=jnp.float32) for t in range(3)
        )
        for j in range(2):
            at = slice(128 * j, 128 * j + 128)
            q2 = jnp.transpose(q4[:, at] * 0.125).astype(jnp.bfloat16)
            v2 = jnp.transpose(v4[:, at]).astype(jnp.bfloat16)
            k2 = k4[:, at]
            turned = pltpu.roll(k2, HEAD, 1)
            first = 4 * g + 2 * j
            send_kv[first, 0] = jnp.where(low, k2[:64], turned[64:]).astype(jnp.bfloat16)
            send_kv[first + 1, 0] = jnp.where(low, turned[:64], k2[64:]).astype(jnp.bfloat16)
            send_kv[first, 1] = v2[:64]
            send_kv[first + 1, 1] = v2[64:]
            send_q[first] = q2[:64]
            send_q[first + 1] = q2[64:]
        for r in range(4):
            head = 4 * g + lax.rem(chip + r, 4)
            if i < 3:
                kv_copy(head, chip).start()
                q_copy(head, chip).start()
            elif r == 0:
                own_kv.start()
                own_pass.start()
                own_q.start()
            else:
                kv_copy(head, chip).start()
                q_copy(head, chip).start()

    def await_meta(i, carry):
        meta_copy(i, lax.rem(me + SEQ - i, SEQ)).wait()
        return carry

    lax.fori_loop(1, SEQ, await_meta, 0)
    own_meta.wait()

    seg = meta_all[:, 0, :]
    dur = meta_all[:, 1, :].astype(jnp.float32)
    lower = (
        lax.broadcasted_iota(jnp.int32, (128, 128), 0)
        <= lax.broadcasted_iota(jnp.int32, (128, 128), 1)
    ).astype(jnp.float32).astype(jnp.bfloat16)
    earlier = (
        lax.broadcasted_iota(jnp.int32, (SEQ, SEQ), 0)
        > lax.broadcasted_iota(jnp.int32, (SEQ, SEQ), 1)
    ).astype(jnp.float32).astype(jnp.bfloat16)
    dur16 = dur.astype(jnp.bfloat16)
    within = jnp.dot(dur16, lower, preferred_element_type=jnp.float32)
    before = jnp.dot(earlier, dur16, preferred_element_type=jnp.float32)
    ends = within + jnp.sum(before, axis=1, keepdims=True)
    seg_ref[...] = seg
    start_ref[...] = (ends - dur).astype(jnp.int32)
    end_ref[...] = ends.astype(jnp.int32)

    first_frame = start_ref[:, 0:1]
    index = lax.broadcasted_iota(jnp.int32, (SEQ, 1), 0)
    late = (index >= 1) & (index <= SEQ - 3) & (first_frame > FRAMES * (index + 1) - 2)
    early = (index >= 3) & (first_frame < FRAMES * (index - 2) + FRAMES + 2)
    far = jnp.sum(jnp.where(late | early, 1.0, 0.0))
    flags[part] = jnp.zeros((8, 128), jnp.float32) + far

    def flag_copy(i, source):
        return pltpu.make_async_remote_copy(
            src_ref=flags.at[source],
            dst_ref=flags.at[source],
            send_sem=flag_send.at[i],
            recv_sem=flag_recv.at[source],
            device_id={"grp": lax.rem(part + i, GROUPS)},
            device_id_type=MESH,
        )

    def send_flag(i, carry):
        flag_copy(i, part).start()
        return carry

    lax.fori_loop(1, GROUPS, send_flag, 0)

    first_seg, last_seg = seg[:, 0:1], seg[:, 127:128]
    lane = lax.broadcasted_iota(jnp.int32, (SEQ, 128), 1)
    lo = jnp.zeros((SEQ, 1), jnp.int32)
    hi = jnp.zeros((SEQ, 1), jnp.int32)
    for s in range(8):
        below = jnp.sum((seg < s).astype(jnp.float32)).astype(jnp.int32)
        upto = jnp.sum((seg <= s).astype(jnp.float32)).astype(jnp.int32)
        lo = jnp.where(first_seg == s, below, lo)
        hi = jnp.where(last_seg == s, upto, hi)
    range_ref[0:SEQ, :] = jnp.where(lane == 0, lo, jnp.where(lane == 1, hi, 0))
    lane8 = lax.broadcasted_iota(jnp.int32, (8, 128), 1)
    block = jnp.zeros((8, 128), jnp.int32)
    for f in range(STEPS):
        t0 = (FRAMES * me + STEP * f - KERNEL // 2).astype(jnp.float32)
        passed = jnp.sum((ends <= t0).astype(jnp.float32)).astype(jnp.int32)
        block = jnp.where(lane8 == f, passed, block)
    range_ref[SEQ : SEQ + 8, :] = block

    def mark(b, carry):
        row = jnp.broadcast_to(meta_all[b, 0:1, :].astype(jnp.float32), (128, 128))
        column = jnp.transpose(row)
        place = lax.broadcasted_iota(jnp.int32, (64, 128), 1).astype(jnp.float32)
        marked = jnp.where(
            place < 8.0,
            jnp.where(place == column[:64], 1.0, 0.0),
            jnp.where(place == column[64:] + 8.0, 1.0, 0.0),
        )
        mark_ref[b] = marked.astype(jnp.bfloat16)
        return carry

    lax.fori_loop(0, SEQ, mark, 0)

    def await_flag(i, carry):
        flag_copy(i, lax.rem(part + GROUPS - i, GROUPS)).wait_recv()
        flag_copy(i, part).wait_send()
        return carry

    lax.fori_loop(1, GROUPS, await_flag, 0)
    total = flags[0]
    for i in range(1, GROUPS):
        total = total + flags[i]
    range_ref[SEQ + 8 :, :] = total.astype(jnp.int32)

    def passing(source):
        return pltpu.make_async_remote_copy(
            src_ref=kv_ref.at[2 * source + core],
            dst_ref=kv_ref.at[2 * source + core],
            send_sem=pass_send.at[source],
            recv_sem=pass_recv.at[source],
            device_id=seq(sibling),
            device_id_type=MESH,
        )

    for i in range(4):
        for r in range(4):
            if i == 3 and r == 0:
                continue
            source = 4 * group_at(own, i) + lax.rem(chip + 4 - r, 4)
            kv_copy(source, source).wait_recv()
            passing(source).start()

    for i in range(4):
        for r in range(4):
            source = 4 * group_at(own, i) + lax.rem(chip + 4 - r, 4)
            if i == 3 and r == 0:
                own_kv.wait()
                own_q.wait()
                own_pass.wait()
            else:
                q_copy(source, source).wait()
                kv_copy(source, source).wait_send()
                passing(source).wait()


def spread(units, gain, meta, w_qkv):
    any_space = pl.BlockSpec(memory_space=pl.ANY)
    vmem = pl.BlockSpec(memory_space=pltpu.VMEM)
    dma = pltpu.SemaphoreType.DMA
    return pl.pallas_call(
        spread_kernel,
        out_shape=(
            jax.ShapeDtypeStruct((SEQ, 2, ROWS // 2, 128), jnp.bfloat16),
            jax.ShapeDtypeStruct((CHIPS, HEAD, 128), jnp.bfloat16),
            jax.ShapeDtypeStruct((SEQ, ROWS // 2, 128), jnp.bfloat16),
            jax.ShapeDtypeStruct((SEQ, 128), jnp.int32),
            jax.ShapeDtypeStruct((SEQ, 128), jnp.int32),
            jax.ShapeDtypeStruct((SEQ, 128), jnp.int32),
            jax.ShapeDtypeStruct((META, 128), jnp.int32),
        ),
        in_specs=[vmem, vmem, vmem, any_space],
        out_specs=(any_space, any_space, vmem, vmem, vmem, vmem, vmem),
        scratch_shapes=[
            pltpu.VMEM((ROWS, WIDTH), jnp.bfloat16),
            pltpu.VMEM((4, 3, WIDTH, 256), jnp.bfloat16),
            pltpu.VMEM((HEADS, 2, ROWS // 2, 128), jnp.bfloat16),
            pltpu.VMEM((HEADS, HEAD, 128), jnp.bfloat16),
            pltpu.VMEM((SEQ, 2, 128), jnp.int32),
            pltpu.VMEM((GROUPS, 8, 128), jnp.float32),
            dma((4, 3)),
            dma((HEADS,)),
            dma((HEADS,)),
            dma((HEADS,)),
            dma((HEADS,)),
            dma((HEADS,)),
            dma((HEADS,)),
            dma((SEQ,)),
            dma((SEQ,)),
            dma((GROUPS,)),
            dma((GROUPS,)),
            dma((3,)),
        ],
        compiler_params=pltpu.CompilerParams(
            collective_id=1, has_side_effects=True, vmem_limit_bytes=16 * MIB
        ),
        name="spread",
    )(units, gain, meta, w_qkv)


def attend_kernel(range_ref, kv_ref, q_ref, mark_ref, seg_ref, out_ref, s_ref):
    core = lax.rem(lax.axis_index("seq"), 2)
    zero = jnp.zeros((64, 256), jnp.bfloat16)
    ones = jnp.ones((16, 128 * BLOCKS), jnp.bfloat16)

    def pair(p, carry):
        first = 4 * p + core
        lo, hi = range_ref[first, 0], range_ref[first + 2, 1]
        lo = lo // 128
        steps = (hi - 128 * lo + 128 * BLOCKS - 1) // (128 * BLOCKS)
        base = jnp.minimum(lo, SEQ - BLOCKS * steps)
        q = jnp.concatenate([q_ref[2 * p], q_ref[2 * p + 1]], axis=1)
        rows = lax.broadcasted_iota(jnp.int32, (8, 128), 0)
        bias = jnp.concatenate(
            [
                jnp.where(seg_ref[pl.ds(first + 2 * e, 1), :] == rows, 0.0, NEG)
                for e in range(2)
            ],
            axis=1,
        )
        none = jnp.zeros((8, 256), jnp.float32)
        biases = jnp.concatenate(
            [
                jnp.concatenate([bias, none], axis=0),
                jnp.concatenate([none, bias], axis=0),
            ],
            axis=1,
        ).astype(jnp.bfloat16)
        right = jnp.concatenate(
            [
                jnp.concatenate([q, zero], axis=1),
                jnp.concatenate([zero, q], axis=1),
                biases,
                jnp.zeros((112, 512), jnp.bfloat16),
            ],
            axis=0,
        )

        def score(i, top):
            block = base + BLOCKS * i
            left = jnp.concatenate(
                [
                    jnp.concatenate([kv_ref[block + t, 0], mark_ref[block + t]], axis=1)
                    for t in range(BLOCKS)
                ],
                axis=0,
            )
            s = jnp.dot(left, right, preferred_element_type=jnp.float32)
            s_ref[i] = s
            return jnp.maximum(top, jnp.max(s.reshape(8 * BLOCKS, 8, 512), axis=0))

        top = lax.fori_loop(0, steps, score, jnp.full((8, 512), NEG, jnp.float32))
        top = jnp.max(jnp.maximum(top[:, :256], top[:, 256:]), axis=0, keepdims=True)
        top = jnp.concatenate([top, top], axis=1)

        def gather(i, acc):
            block = base + BLOCKS * i
            w = jnp.exp(s_ref[i] - top).astype(jnp.bfloat16)
            wt = jnp.concatenate(
                [w[64 * t : 64 * t + 64, 256 * h : 256 * h + 256] for t in range(BLOCKS) for h in range(2)], axis=0
            )
            vt = jnp.concatenate([kv_ref[block + t, 1] for t in range(BLOCKS)], axis=1)
            vt = jnp.concatenate([vt, ones], axis=0)
            return acc + jnp.dot(vt, wt, preferred_element_type=jnp.float32)

        acc = lax.fori_loop(0, steps, gather, jnp.zeros((80, 256), jnp.float32))
        out = (acc[:64] / acc[64:65]).astype(jnp.bfloat16)
        out_ref[2 * p] = out[:, :128]
        out_ref[2 * p + 1] = out[:, 128:]
        return carry

    lax.fori_loop(0, CHIPS // 2, pair, 0)

def attend(ranges, kv, q, marks, seg):
    vmem = pl.BlockSpec(memory_space=pltpu.VMEM)
    return pl.pallas_call(
        attend_kernel,
        out_shape=jax.ShapeDtypeStruct((CHIPS, HEAD, 128), jnp.bfloat16),
        in_specs=[pl.BlockSpec(memory_space=pltpu.SMEM), vmem, vmem, vmem, vmem],
        out_specs=vmem,
        scratch_shapes=[pltpu.VMEM((SEQ // BLOCKS, 64 * BLOCKS, 512), jnp.float32)],
        compiler_params=pltpu.CompilerParams(vmem_limit_bytes=16 * MIB),
        name="attend",
    )(ranges, kv, q, marks, seg)


def send_back(o_ref, landed, o_send, o_recv, own_sem, me):
    core = lax.rem(me, 2)
    chip = me // 2

    def o_copy(target, source):
        return pltpu.make_async_remote_copy(
            src_ref=o_ref.at[target],
            dst_ref=landed.at[source],
            send_sem=o_send.at[target],
            recv_sem=o_recv.at[source],
            device_id=seq(2 * target + core),
            device_id_type=MESH,
        )

    def send(i, carry):
        o_copy(lax.rem(chip + i, CHIPS), chip).start()
        return carry

    lax.fori_loop(1, CHIPS, send, 0)
    own = pltpu.make_async_copy(o_ref.at[chip], landed.at[chip], own_sem)
    own.start()

    def receive(i, carry):
        source = lax.rem(chip + CHIPS - i, CHIPS)
        o_copy(source, source).wait()
        return carry

    lax.fori_loop(1, CHIPS, receive, 0)
    own.wait()


def project(landed, units_ref, w_out, w_proj):
    turned = [
        jnp.transpose(
            jnp.concatenate([landed[2 * j], landed[2 * j + 1]], axis=0).astype(jnp.float32)
        ).astype(jnp.bfloat16)
        for j in range(HEADS // 2)
    ]
    attended = jnp.concatenate(turned, axis=1)
    mixed = jnp.dot(attended, w_out, preferred_element_type=jnp.float32)
    mixed = (mixed + units_ref[...].astype(jnp.float32)).astype(jnp.bfloat16)
    return jnp.dot(mixed, w_proj, preferred_element_type=jnp.float32).astype(jnp.bfloat16)


def make_frames(
    me, base, last, range_ref, window_ref, start_ref, end_ref, w_ref, b_ref, gain_ref, out_ref, stacked
):
    for f in range(STEPS):
        block = jnp.clip(range_ref[SEQ, f] // 128, base, last)
        starts = jnp.concatenate(
            [start_ref[pl.ds(block, 1), :], start_ref[pl.ds(block + 1, 1), :]], axis=1
        )
        ends = jnp.concatenate(
            [end_ref[pl.ds(block, 1), :], end_ref[pl.ds(block + 1, 1), :]], axis=1
        )
        window = window_ref[pl.ds(block - base, 2)].reshape(256, CHANNELS)
        frame = lax.broadcasted_iota(jnp.int32, (STEP, 256), 0)
        first = FRAMES * me + STEP * f - KERNEL // 2
        starts, ends = starts - first, ends - first
        for j in range(KERNEL):
            chosen = jnp.where((frame >= starts - j) & (frame < ends - j), 1.0, 0.0)
            rows = jnp.dot(
                chosen.astype(jnp.bfloat16), window, preferred_element_type=jnp.float32
            )
            stacked[STEP * f : STEP * f + STEP, CHANNELS * j : CHANNELS * j + CHANNELS] = (
                rows.astype(jnp.bfloat16)
            )
    bias, gain = b_ref[...], gain_ref[...]
    for r in range(FRAMES // TILE):
        at = slice(TILE * r, TILE * r + TILE)
        conv = jnp.dot(stacked[at, :], w_ref[...], preferred_element_type=jnp.float32) + bias
        value = jnp.maximum(conv, 0.0)
        mean = jnp.mean(value, axis=-1, keepdims=True)
        centred = value - mean
        variance = jnp.mean(centred * centred, axis=-1, keepdims=True)
        half = KERNEL // 2
        centre = stacked[at, half * CHANNELS : (half + 1) * CHANNELS].astype(jnp.float32)
        result = centre + centred / jnp.sqrt(variance + 1e-05) * gain
        out_ref[at, :] = result.astype(jnp.bfloat16)


def finish_near_kernel(
    range_ref,
    o_ref,
    units_ref,
    w_out_ref,
    w_proj_ref,
    start_ref,
    end_ref,
    w_ref,
    b_ref,
    gain_ref,
    out_ref,
    landed,
    w_out,
    w_proj,
    conv_w,
    window,
    stacked,
    o_send,
    o_recv,
    near_send,
    near_recv,
    w_sem,
    own_sem,
):
    me = lax.axis_index("seq")
    greet_all(me)
    loads = [
        pltpu.make_async_copy(a, b, w_sem.at[i])
        for i, (a, b) in enumerate(((w_out_ref, w_out), (w_proj_ref, w_proj), (w_ref, conv_w)))
    ]
    for load in loads:
        load.start()
    await_all()
    send_back(o_ref, landed, o_send, o_recv, own_sem, me)
    loads[0].wait()
    loads[1].wait()

    def base_of(device):
        return jnp.clip(device - 1, 0, SEQ - 3)

    base = base_of(me)
    window[me - base] = project(landed, units_ref, w_out[...], w_proj[...])

    def near_copy(i, source, target):
        slot = source - base_of(target)
        return pltpu.make_async_remote_copy(
            src_ref=window.at[me - base],
            dst_ref=window.at[slot],
            send_sem=near_send.at[i],
            recv_sem=near_recv.at[slot],
            device_id=seq(target),
            device_id_type=MESH,
        )

    routes = (
        (me > 0, lax.rem(me + SEQ - 1, SEQ)),
        (me < SEQ - 1, lax.rem(me + 1, SEQ)),
        (me == 2, 0),
        (me == SEQ - 3, SEQ - 1),
    )
    for i, (present, target) in enumerate(routes):

        @pl.when(present)
        def _():
            near_copy(i, me, target).start()

    for slot in range(3):

        @pl.when(slot != me - base)
        def _():
            pltpu.make_async_remote_copy(
                src_ref=window.at[slot],
                dst_ref=window.at[slot],
                send_sem=near_send.at[0],
                recv_sem=near_recv.at[slot],
                device_id=seq(lax.rem(me + 1, SEQ)),
                device_id_type=MESH,
            ).wait_recv()

    loads[2].wait()
    make_frames(
        me, base, base + 1, range_ref, window, start_ref, end_ref, conv_w, b_ref, gain_ref, out_ref, stacked
    )
    for i, (present, target) in enumerate(routes):

        @pl.when(present)
        def _():
            near_copy(i, me, target).wait_send()


def finish_near(ranges, o, units, w_out, w_proj, starts, ends, conv_w, conv_b, conv_gain):
    vmem = pl.BlockSpec(memory_space=pltpu.VMEM)
    any_space = pl.BlockSpec(memory_space=pl.ANY)
    dma = pltpu.SemaphoreType.DMA
    return pl.pallas_call(
        finish_near_kernel,
        out_shape=jax.ShapeDtypeStruct((FRAMES, CHANNELS), jnp.bfloat16),
        in_specs=[pl.BlockSpec(memory_space=pltpu.SMEM), vmem, vmem, any_space, any_space]
        + [vmem, vmem, any_space, vmem, vmem],
        out_specs=vmem,
        scratch_shapes=[
            pltpu.VMEM((HEADS, HEAD, 128), jnp.bfloat16),
            pltpu.VMEM((WIDTH, WIDTH), jnp.bfloat16),
            pltpu.VMEM((WIDTH, CHANNELS), jnp.bfloat16),
            pltpu.VMEM((KERNEL * CHANNELS, CHANNELS), jnp.bfloat16),
            pltpu.VMEM((3, ROWS, CHANNELS), jnp.bfloat16),
            pltpu.VMEM((FRAMES, KERNEL * CHANNELS), jnp.bfloat16),
            dma((CHIPS,)),
            dma((CHIPS,)),
            dma((4,)),
            dma((3,)),
            dma((3,)),
            dma,
        ],
        compiler_params=pltpu.CompilerParams(
            collective_id=2, has_side_effects=True, vmem_limit_bytes=32 * MIB
        ),
        name="finish_near",
    )(ranges, o, units, w_out, w_proj, starts, ends, conv_w, conv_b, conv_gain)


def mix_kernel(
    o_ref, units_ref, w_out_ref, w_proj_ref, out_ref, landed, o_send, o_recv, own_sem
):
    me = lax.axis_index("seq")
    greet_all(me)
    await_all()
    send_back(o_ref, landed, o_send, o_recv, own_sem, me)
    out_ref[...] = project(landed, units_ref, w_out_ref[...], w_proj_ref[...])


def mix(o, units, w_out, w_proj):
    vmem = pl.BlockSpec(memory_space=pltpu.VMEM)
    dma = pltpu.SemaphoreType.DMA
    return pl.pallas_call(
        mix_kernel,
        out_shape=jax.ShapeDtypeStruct((ROWS, CHANNELS), jnp.bfloat16),
        in_specs=[vmem] * 4,
        out_specs=vmem,
        scratch_shapes=[
            pltpu.VMEM((HEADS, HEAD, 128), jnp.bfloat16),
            dma((CHIPS,)),
            dma((CHIPS,)),
            dma,
        ],
        compiler_params=pltpu.CompilerParams(
            collective_id=3, has_side_effects=True, vmem_limit_bytes=16 * MIB
        ),
        name="mix",
    )(o, units, w_out, w_proj)


def gather_kernel(block_ref, whole_ref, send_sem, recv_sem, own_sem):
    me = lax.axis_index("seq")
    greet_all(me)
    await_all()

    def copy(i, source):
        return pltpu.make_async_remote_copy(
            src_ref=block_ref,
            dst_ref=whole_ref.at[source],
            send_sem=send_sem.at[i],
            recv_sem=recv_sem.at[source],
            device_id=seq(lax.rem(me + i, SEQ)),
            device_id_type=MESH,
        )

    def send(i, carry):
        copy(i, me).start()
        return carry

    def receive(i, carry):
        copy(i, lax.rem(me + SEQ - i, SEQ)).wait()
        return carry

    lax.fori_loop(1, SEQ, send, 0)
    own = pltpu.make_async_copy(block_ref, whole_ref.at[me], own_sem)
    own.start()
    lax.fori_loop(1, SEQ, receive, 0)
    own.wait()


def gather(reduced):
    any_space = pl.BlockSpec(memory_space=pl.ANY)
    dma = pltpu.SemaphoreType.DMA
    return pl.pallas_call(
        gather_kernel,
        out_shape=jax.ShapeDtypeStruct((SEQ, ROWS, CHANNELS), jnp.bfloat16),
        in_specs=[any_space],
        out_specs=any_space,
        scratch_shapes=[dma((SEQ,)), dma((SEQ,)), dma],
        compiler_params=pltpu.CompilerParams(collective_id=4, has_side_effects=True),
        name="gather",
    )(reduced)


def frames_kernel(
    range_ref, whole_ref, start_ref, end_ref, w_ref, b_ref, gain_ref, out_ref, stacked
):
    make_frames(
        lax.axis_index("seq"),
        0,
        SEQ - 2,
        range_ref,
        whole_ref,
        start_ref,
        end_ref,
        w_ref,
        b_ref,
        gain_ref,
        out_ref,
        stacked,
    )


def frames(ranges, whole, starts, ends, conv_w, conv_b, conv_gain):
    vmem = pl.BlockSpec(memory_space=pltpu.VMEM)
    return pl.pallas_call(
        frames_kernel,
        out_shape=jax.ShapeDtypeStruct((FRAMES, CHANNELS), jnp.bfloat16),
        in_specs=[pl.BlockSpec(memory_space=pltpu.SMEM)] + [vmem] * 6,
        out_specs=vmem,
        scratch_shapes=[pltpu.VMEM((FRAMES, KERNEL * CHANNELS), jnp.bfloat16)],
        compiler_params=pltpu.CompilerParams(vmem_limit_bytes=32 * MIB),
        name="frames",
    )(ranges, whole, starts, ends, conv_w, conv_b, conv_gain)


def finish_far(ranges, o, units, w_out, w_proj, starts, ends, conv_w, conv_b, conv_gain):
    whole = gather(mix(o, units, w_out, w_proj))
    return frames(ranges, whole, starts, ends, conv_w, conv_b, conv_gain)


def local(units, durations, seg_ids, ln_gain, w_qkv, w_out, w_proj, conv_w, conv_b, conv_gain):
    meta = jnp.stack([seg_ids, durations])
    kv, q, marks, seg, starts, ends, ranges = spread(
        units, ln_gain.reshape(1, WIDTH), meta, w_qkv
    )
    o = attend(ranges, kv, q, marks, seg)
    return lax.cond(
        ranges[SEQ + 8, 0] == 0,
        finish_near,
        finish_far,
        ranges,
        o,
        units,
        w_out,
        w_proj,
        starts,
        ends,
        conv_w.reshape(KERNEL * CHANNELS, CHANNELS),
        conv_b.reshape(1, CHANNELS),
        conv_gain.reshape(1, CHANNELS),
    )


def solution(mesh):
    parted = P(("grp", "seq"))
    wide = P(("grp", "seq"), None)
    return jax.shard_map(
        local,
        mesh=mesh,
        in_specs=(wide, parted, parted) + (P(),) * 7,
        out_specs=wide,
        check_vma=False,
    )
```

time: 188 us -> 80.7 us (0.43)
  the two profiles are of different devices: /device:TPU:1 before, /device:TPU:4 now
where the time goes in v2:
time: 80.7 us; the launch traced here: 80.5 us
  Pallas kernels  73.3 us (91%)
  local copies, waits for them, and re-layouts  5.65 us (7%)
    pallas_call x1, Pallas kernels, spread(): pl.pallas_call(spread_kernel, out_shape=(jax.ShapeDtypeStruct((SEQ, 2, RO...  33.3 us
    pallas_call x1, Pallas kernels, finish_near(): pl.pallas_call(finish_near_kernel, out_shape=jax.ShapeDtypeStruct((FRAMES...  27.5 us
    pallas_call x1, Pallas kernels, attend(): pl.pallas_call(attend_kernel, out_shape=jax.ShapeDtypeStruct((CHIPS, HEAD...  12.4 us
    unnamed x13, local copies, waits for them, and re-layouts  4.37 us

profile of v2, /device:TPU:4, one launch (start us, length us, event | category | flops | bytes accessed | tf_op | source)
XLA Modules:
  0.0 80.5 jit_solution(14091190244549210260)
XLA Ops:
  0.0 0.7 pad_add_fusion.meta_ref
  0.7 0.0 copy-start.1
  0.7 2.8 %copy-done.1 = bf16[1024,3072]{1,0:T(8,128)(2,1)S(1)} copy-done((bf16[1024,3072]{1,0:T(8,128)(2,1)S(1)}, bf16[1024,3072]{1,0:T(8,128)(2,1)}, u32[]{:S(2)}) %copy-start.1) | copy-done | bytes 6291480
  3.5 0.0 copy-start.3
  3.5 0.7 copy-done.3
  4.2 0.0 copy-start.4
  4.2 0.0 copy-start.5
  4.2 0.0 copy-start.8
  4.2 0.0 copy-start.9
  4.2 33.3 %spread.1 = (bf16[32,2,64,128]{3,2,1,0:T(8,128)(2,1)S(1)}, bf16[16,64,128]{2,1,0:T(8,128)(2,1)S(1)}, bf16[32,64,128]{2,1,0:T(8,128)(2,1)S(1)}, s32[32,128]{1,0:T...) custom-call(bf16[128,1024]{1,0:T(8,128)(2,1)} %units_ref.1, ...), custom_call_target="tpu_custom_call" | custom-call | tf_op jit(solution)/shard_map/spread/pallas_call | solution.py:344
  37.5 0.5 slice.3
  38.7 12.4 %attend.1 = bf16[16,64,128]{2,1,0:T(8,128)(2,1)S(1)} custom-call(s32[48,128]{1,0:T(8,128)S(1)} %get-tuple-element.75.range_ref, bf16[32,2,64,128]{3,2,1,0:T(8,128)(2,1)S(1)} %get-tuple-element.76.kv_ref, bf16[16,64,128]{2,1,0:T(8,128)(2,1)S(1)} %get-tuple-element.77.q_ref, bf16[32,64,128]{2,1,0:T(8,128)(2,1)S(1)} %get-tuple-element.78.mark_ref, ...), custom_call_target="tpu_custom_call" | custom-call | tf_op jit(solution)/shard_map/attend/pallas_call | solution.py:459
  51.1 0.0 copy-done.4
  51.1 0.0 copy-done.5
  51.1 0.0 copy-done.8
  51.1 0.0 copy-done.9
  51.1 28.5 %conditional.1 = (bf16[768,512]{1,0:T(8,128)(2,1)S(1)}) conditional(s32[]{:T(128)} %bitcast.3, (bf16[16,64,128]{2,1,0:T(8,128)(2,1)S(1)}, bf16[128,1024]{1,0:T(8,128)(2,1)S(1)}, bf16[1024,1024]{1,0:T(8,128)(2,1)}, bf16[1024,512]{1,0:T(8,128)(2,1)}, s32[48,128]{1,0:T(8,128)S(1)}, /*index=5*/s32[32,128]{1,0:T(8,128)S(1)}, s32[32,128]{1,0:T(8,128)S(1)}, ...), branch_computations={%region_0.0_spmd, %region_1.0_spmd} | conditional | bytes 17301568 | solution.py:791
  51.4 0.0 copy-start.6
  51.4 0.0 copy-start.7
  51.4 0.7 copy-done.6
  52.0 0.1 copy-done.7
  52.1 27.5 %finish_near.1 = bf16[768,512]{1,0:T(8,128)(2,1)S(1)} custom-call(s32[48,128]{1,0:T(8,128)S(1)} %get-tuple-element.58.range_ref, bf16[16,64,128]{2,1,0:T(8,128)(2,1)} %copy-done.7, bf16[128,1024]{1,0:T(8,128)(2,1)} %copy-done.6, bf16[1024,1024]{1,0:T(8,128)(2,1)} %get-tuple-element.61.w_out_ref, bf16[1024,512]{1,0:T(8,128)(2,1)} %get-tuple-element.62.w_proj_ref, ...), custom_call_target="tpu_custom_call" | custom-call | tf_op jit(solution)/shard_map/cond/branch_1_fun/finish_near/pallas_call | solution.py:646
  79.6 0.9 %copy.16 = bf16[768,512]{1,0:T(8,128)(2,1)} copy(bf16[768,512]{1,0:T(8,128)(2,1)S(1)} %get-tuple-element.82) | data formatting | bytes 1572864
Async XLA Ops:
  0.7 2.8 %copy-start.1 = (bf16[1024,3072]{1,0:T(8,128)(2,1)S(1)}, bf16[1024,3072]{1,0:T(8,128)(2,1)}, u32[]{:S(2)}) copy-start(bf16[1024,3072]{1,0:T(8,128)(2,1)} %w_ref.1) | copy-start | bytes 18874372
  3.5 0.7 copy-start.3
  4.2 47.0 %copy-start.4 = (bf16[5,512,512]{2,1,0:T(8,128)(2,1)S(1)}, bf16[5,512,512]{2,1,0:T(8,128)(2,1)}, u32[]{:S(2)}) copy-start(bf16[5,512,512]{2,1,0:T(8,128)(2,1)} %param.19) | copy-start | bytes 7864324
  4.2 47.0 %copy-start.5 = (bf16[128,1024]{1,0:T(8,128)(2,1)S(1)}, bf16[128,1024]{1,0:T(8,128)(2,1)}, u32[]{:S(2)}) copy-start(bf16[128,1024]{1,0:T(8,128)(2,1)} %units_ref.1) | copy-start | bytes 786436
  4.2 47.0 %copy-start.8 = (f32[512]{0:T(512)S(1)}, f32[512]{0:T(512)}, u32[]{:S(2)}) copy-start(f32[512]{0:T(512)} %param.20) | copy-start | bytes 6148
  4.2 47.0 %copy-start.9 = (f32[512]{0:T(512)S(1)}, f32[512]{0:T(512)}, u32[]{:S(2)}) copy-start(f32[512]{0:T(512)} %param.21) | copy-start | bytes 6148
  51.4 0.7 copy-start.6
  51.4 0.8 copy-start.7

commit v3 on v2

--- a/solution.py
+++ b/solution.py
@@ -25,6 +25,7 @@
 GROUPS = 8
 NEG = -1e30
 MIB = 1024 * 1024
+SPREAD_MIB = 56
 META = SEQ + 16
 
 
@@ -32,20 +33,30 @@
     return {"seq": index}
 
 
+def greet(device):
+    pl.semaphore_signal(
+        pltpu.get_barrier_semaphore(), 1, device_id=device, device_id_type=MESH
+    )
+
+
 def greet_all(me):
-    barrier = pltpu.get_barrier_semaphore()
-
-    def greet(i, carry):
-        pl.semaphore_signal(
-            barrier, 1, device_id=seq(lax.rem(me + i, SEQ)), device_id_type=MESH
-        )
-        return carry
-
-    lax.fori_loop(1, SEQ, greet, 0)
-
-
-def await_all(more=0):
-    pl.semaphore_wait(pltpu.get_barrier_semaphore(), SEQ - 1 + more)
+    def one(i, carry):
+        greet(seq(lax.rem(me + i, SEQ)))
+        return carry
+
+    lax.fori_loop(1, SEQ, one, 0)
+
+
+def greet_row(me):
+    def one(i, carry):
+        greet(seq(lax.rem(me + 2 * i, SEQ)))
+        return carry
+
+    lax.fori_loop(1, CHIPS, one, 0)
+
+
+def await_greetings(count):
+    pl.semaphore_wait(pltpu.get_barrier_semaphore(), count)
 
 
 def group_at(own, i):
@@ -100,15 +111,11 @@
     chip = me // 2
     sibling = me + 1 - 2 * core
     own = chip // 4
-    greet_all(me)
+    greet_row(me)
+    greet(seq(sibling))
 
     def greet_part(i, carry):
-        pl.semaphore_signal(
-            pltpu.get_barrier_semaphore(),
-            1,
-            device_id={"grp": lax.rem(part + i, GROUPS)},
-            device_id_type=MESH,
-        )
+        greet({"grp": lax.rem(part + i, GROUPS)})
         return carry
 
     lax.fori_loop(1, GROUPS, greet_part, 0)
@@ -120,8 +127,10 @@
         )
 
     for i in range(4):
-        for t in range(3):
-            w_copy(i, t).start()
+        w_copy(i, 1).start()
+        w_copy(i, 2).start()
+    for i in range(4):
+        w_copy(i, 0).start()
 
     x = units_ref[...].astype(jnp.float32)
     mean = jnp.mean(x, axis=-1, keepdims=True)
@@ -129,25 +138,29 @@
     variance = jnp.mean(centred * centred, axis=-1, keepdims=True)
     h_ref[...] = (centred / jnp.sqrt(variance + 1e-05) * gain_ref[...]).astype(jnp.bfloat16)
 
-    await_all(GROUPS - 1)
-
     def meta_copy(i, source):
         return pltpu.make_async_remote_copy(
             src_ref=meta_ref,
-            dst_ref=meta_all.at[source],
+            dst_ref=meta_all.at[source, core],
             send_sem=meta_send.at[i],
             recv_sem=meta_recv.at[source],
-            device_id=seq(lax.rem(me + i, SEQ)),
+            device_id=seq(lax.rem(me + 2 * i, SEQ)),
             device_id_type=MESH,
         )
 
     def send_meta(i, carry):
-        meta_copy(i, me).start()
-        return carry
-
-    lax.fori_loop(1, SEQ, send_meta, 0)
-    own_meta = pltpu.make_async_copy(meta_ref, meta_all.at[me], own_sem.at[2])
-    own_meta.start()
+        meta_copy(i, chip).start()
+        return carry
+
+    own_meta = pltpu.make_async_copy(meta_ref, meta_all.at[chip, core], own_sem.at[2])
+    pass_meta = pltpu.make_async_remote_copy(
+        src_ref=meta_all.at[:, core],
+        dst_ref=meta_all.at[:, core],
+        send_sem=meta_send.at[0],
+        recv_sem=own_sem.at[3],
+        device_id=seq(sibling),
+        device_id_type=MESH,
+    )
 
     def kv_copy(head, source):
         return pltpu.make_async_remote_copy(
@@ -183,15 +196,14 @@
     low = low_lanes(ROWS // 2)
     for i in range(4):
         g = group_at(own, i)
-        for t in range(3):
-            w_copy(i, t).wait()
+        w_copy(i, 1).wait()
+        w_copy(i, 2).wait()
         h = h_ref[...]
-        q4, k4, v4 = (
-            jnp.dot(h, wbuf[i, t], preferred_element_type=jnp.float32) for t in range(3)
+        k4, v4 = (
+            jnp.dot(h, wbuf[i, t], preferred_element_type=jnp.float32) for t in (1, 2)
         )
         for j in range(2):
             at = slice(128 * j, 128 * j + 128)
-            q2 = jnp.transpose(q4[:, at] * 0.125).astype(jnp.bfloat16)
             v2 = jnp.transpose(v4[:, at]).astype(jnp.bfloat16)
             k2 = k4[:, at]
             turned = pltpu.roll(k2, HEAD, 1)
@@ -200,30 +212,44 @@
             send_kv[first + 1, 0] = jnp.where(low, turned[:64], k2[64:]).astype(jnp.bfloat16)
             send_kv[first, 1] = v2[:64]
             send_kv[first + 1, 1] = v2[64:]
+        if i == 0:
+            await_greetings(CHIPS - 1 + 1 + GROUPS - 1)
+        for r in range(4):
+            if i == 3 and r == 0:
+                own_kv.start()
+                own_pass.start()
+            else:
+                kv_copy(4 * g + lax.rem(chip + r, 4), chip).start()
+        if i == 0:
+            lax.fori_loop(1, CHIPS, send_meta, 0)
+            own_meta.start()
+    for i in range(4):
+        g = group_at(own, i)
+        w_copy(i, 0).wait()
+        q4 = jnp.dot(h_ref[...], wbuf[i, 0], preferred_element_type=jnp.float32) * 0.125
+        for j in range(2):
+            q2 = jnp.transpose(q4[:, 128 * j : 128 * j + 128]).astype(jnp.bfloat16)
+            first = 4 * g + 2 * j
             send_q[first] = q2[:64]
             send_q[first + 1] = q2[64:]
         for r in range(4):
-            head = 4 * g + lax.rem(chip + r, 4)
-            if i < 3:
-                kv_copy(head, chip).start()
-                q_copy(head, chip).start()
-            elif r == 0:
-                own_kv.start()
-                own_pass.start()
+            if i == 3 and r == 0:
                 own_q.start()
             else:
-                kv_copy(head, chip).start()
-                q_copy(head, chip).start()
+                q_copy(4 * g + lax.rem(chip + r, 4), chip).start()
 
     def await_meta(i, carry):
-        meta_copy(i, lax.rem(me + SEQ - i, SEQ)).wait()
-        return carry
-
-    lax.fori_loop(1, SEQ, await_meta, 0)
+        meta_copy(i, lax.rem(chip + CHIPS - i, CHIPS)).wait()
+        return carry
+
+    lax.fori_loop(1, CHIPS, await_meta, 0)
     own_meta.wait()
-
-    seg = meta_all[:, 0, :]
-    dur = meta_all[:, 1, :].astype(jnp.float32)
+    pass_meta.start()
+    pass_meta.wait()
+    meta = meta_all[...].reshape(SEQ, 2, 128)
+
+    seg = meta[:, 0, :]
+    dur = meta[:, 1, :].astype(jnp.float32)
     lower = (
         lax.broadcasted_iota(jnp.int32, (128, 128), 0)
         <= lax.broadcasted_iota(jnp.int32, (128, 128), 1)
@@ -282,7 +308,7 @@
     range_ref[SEQ : SEQ + 8, :] = block
 
     def mark(b, carry):
-        row = jnp.broadcast_to(meta_all[b, 0:1, :].astype(jnp.float32), (128, 128))
+        row = jnp.broadcast_to(seg_ref[pl.ds(b, 1), :].astype(jnp.float32), (128, 128))
         column = jnp.transpose(row)
         place = lax.broadcasted_iota(jnp.int32, (64, 128), 1).astype(jnp.float32)
         marked = jnp.where(
@@ -359,7 +385,7 @@
             pltpu.VMEM((4, 3, WIDTH, 256), jnp.bfloat16),
             pltpu.VMEM((HEADS, 2, ROWS // 2, 128), jnp.bfloat16),
             pltpu.VMEM((HEADS, HEAD, 128), jnp.bfloat16),
-            pltpu.VMEM((SEQ, 2, 128), jnp.int32),
+            pltpu.VMEM((CHIPS, 2, 2, 128), jnp.int32),
             pltpu.VMEM((GROUPS, 8, 128), jnp.float32),
             dma((4, 3)),
             dma((HEADS,)),
@@ -368,31 +394,34 @@
             dma((HEADS,)),
             dma((HEADS,)),
             dma((HEADS,)),
-            dma((SEQ,)),
-            dma((SEQ,)),
+            dma((CHIPS,)),
+            dma((CHIPS,)),
             dma((GROUPS,)),
             dma((GROUPS,)),
-            dma((3,)),
+            dma((4,)),
         ],
         compiler_params=pltpu.CompilerParams(
-            collective_id=1, has_side_effects=True, vmem_limit_bytes=16 * MIB
+            collective_id=1, has_side_effects=True, vmem_limit_bytes=SPREAD_MIB * MIB
         ),
         name="spread",
     )(units, gain, meta, w_qkv)
 
 
-def attend_kernel(range_ref, kv_ref, q_ref, mark_ref, seg_ref, out_ref, s_ref):
+def attend_kernel(range_ref, kv_ref, q_ref, mark_ref, seg_ref, out_ref, even_ref, odd_ref):
     core = lax.rem(lax.axis_index("seq"), 2)
-    zero = jnp.zeros((64, 256), jnp.bfloat16)
+    pairs = CHIPS // 2
     ones = jnp.ones((16, 128 * BLOCKS), jnp.bfloat16)
 
-    def pair(p, carry):
+    def extent(p):
         first = 4 * p + core
-        lo, hi = range_ref[first, 0], range_ref[first + 2, 1]
-        lo = lo // 128
+        lo, hi = range_ref[first, 0] // 128, range_ref[first + 2, 1]
         steps = (hi - 128 * lo + 128 * BLOCKS - 1) // (128 * BLOCKS)
-        base = jnp.minimum(lo, SEQ - BLOCKS * steps)
+        return jnp.minimum(lo, SEQ - BLOCKS * steps), steps
+
+    def right_side(p):
+        first = 4 * p + core
         q = jnp.concatenate([q_ref[2 * p], q_ref[2 * p + 1]], axis=1)
+        zero = jnp.zeros((HEAD, 256), jnp.bfloat16)
         rows = lax.broadcasted_iota(jnp.int32, (8, 128), 0)
         bias = jnp.concatenate(
             [
@@ -403,13 +432,10 @@
         )
         none = jnp.zeros((8, 256), jnp.float32)
         biases = jnp.concatenate(
-            [
-                jnp.concatenate([bias, none], axis=0),
-                jnp.concatenate([none, bias], axis=0),
-            ],
+            [jnp.concatenate([bias, none], axis=0), jnp.concatenate([none, bias], axis=0)],
             axis=1,
         ).astype(jnp.bfloat16)
-        right = jnp.concatenate(
+        return jnp.concatenate(
             [
                 jnp.concatenate([q, zero], axis=1),
                 jnp.concatenate([zero, q], axis=1),
@@ -419,40 +445,87 @@
             axis=0,
         )
 
-        def score(i, top):
-            block = base + BLOCKS * i
-            left = jnp.concatenate(
-                [
-                    jnp.concatenate([kv_ref[block + t, 0], mark_ref[block + t]], axis=1)
-                    for t in range(BLOCKS)
-                ],
-                axis=0,
-            )
-            s = jnp.dot(left, right, preferred_element_type=jnp.float32)
-            s_ref[i] = s
-            return jnp.maximum(top, jnp.max(s.reshape(8 * BLOCKS, 8, 512), axis=0))
-
-        top = lax.fori_loop(0, steps, score, jnp.full((8, 512), NEG, jnp.float32))
+    def score(right, block, keep, top):
+        left = jnp.concatenate(
+            [
+                jnp.concatenate([kv_ref[block + t, 0], mark_ref[block + t]], axis=1)
+                for t in range(BLOCKS)
+            ],
+            axis=0,
+        )
+        s = jnp.dot(left, right, preferred_element_type=jnp.float32)
+        keep[...] = s
+        return jnp.maximum(top, jnp.max(s.reshape(8 * BLOCKS, 8, 512), axis=0))
+
+    def collect(top, block, kept, acc):
+        w = jnp.exp(kept[...] - top).astype(jnp.bfloat16)
+        w = jnp.concatenate(
+            [
+                w[64 * t : 64 * t + 64, 256 * h : 256 * h + 256]
+                for t in range(BLOCKS)
+                for h in range(2)
+            ],
+            axis=0,
+        )
+        v = jnp.concatenate([kv_ref[block + t, 1] for t in range(BLOCKS)], axis=1)
+        v = jnp.concatenate([v, ones], axis=0)
+        return acc + jnp.dot(v, w, preferred_element_type=jnp.float32)
+
+    def peak(top):
         top = jnp.max(jnp.maximum(top[:, :256], top[:, 256:]), axis=0, keepdims=True)
-        top = jnp.concatenate([top, top], axis=1)
-
-        def gather(i, acc):
-            block = base + BLOCKS * i
-            w = jnp.exp(s_ref[i] - top).astype(jnp.bfloat16)
-            wt = jnp.concatenate(
-                [w[64 * t : 64 * t + 64, 256 * h : 256 * h + 256] for t in range(BLOCKS) for h in range(2)], axis=0
-            )
-            vt = jnp.concatenate([kv_ref[block + t, 1] for t in range(BLOCKS)], axis=1)
-            vt = jnp.concatenate([vt, ones], axis=0)
-            return acc + jnp.dot(vt, wt, preferred_element_type=jnp.float32)
-
-        acc = lax.fori_loop(0, steps, gather, jnp.zeros((80, 256), jnp.float32))
-        out = (acc[:64] / acc[64:65]).astype(jnp.bfloat16)
+        return jnp.concatenate([top, top], axis=1)
+
+    def give(p, acc):
+        out = (acc[:HEAD] / acc[HEAD : HEAD + 1]).astype(jnp.bfloat16)
         out_ref[2 * p] = out[:, :128]
         out_ref[2 * p + 1] = out[:, 128:]
-        return carry
-
-    lax.fori_loop(0, CHIPS // 2, pair, 0)
+
+    low = jnp.full((8, 512), NEG, jnp.float32)
+    clear = jnp.zeros((HEAD + 16, 256), jnp.float32)
+    base0, steps0 = extent(0)
+    right0 = right_side(0)
+    top0 = lax.fori_loop(
+        0, steps0, lambda i, top: score(right0, base0 + BLOCKS * i, even_ref.at[i], top), low
+    )
+
+    def both(p, here, there, top):
+        base, steps = extent(p)
+        old_base, old_steps = extent(p - 1)
+        right = right_side(p)
+
+        def run(count):
+            new_top, acc = low, clear
+            for i in range(count):
+                j = jnp.minimum(i, steps - 1)
+                new_top = score(right, base + BLOCKS * j, here.at[j], new_top)
+                k = jnp.minimum(i, old_steps - 1)
+                level = jnp.where(i < old_steps, top, -NEG)
+                acc = collect(level, old_base + BLOCKS * k, there.at[k], acc)
+            return new_top, acc
+
+        new_top, acc = lax.switch(
+            jnp.maximum(steps, old_steps) - 1,
+            [functools.partial(run, count + 1) for count in range(SEQ // BLOCKS)],
+        )
+        give(p - 1, acc)
+        return peak(new_top)
+
+    def two(i, top):
+        top = both(2 * i + 1, odd_ref, even_ref, top)
+        return both(2 * i + 2, even_ref, odd_ref, top)
+
+    top = lax.fori_loop(0, pairs // 2 - 1, two, peak(top0))
+    top = both(pairs - 1, odd_ref, even_ref, top)
+    last = pairs - 1
+    base, steps = extent(last)
+    acc = lax.fori_loop(
+        0,
+        steps,
+        lambda i, acc: collect(top, base + BLOCKS * i, odd_ref.at[i], acc),
+        clear,
+    )
+    give(last, acc)
+
 
 def attend(ranges, kv, q, marks, seg):
     vmem = pl.BlockSpec(memory_space=pltpu.VMEM)
@@ -461,8 +534,8 @@
         out_shape=jax.ShapeDtypeStruct((CHIPS, HEAD, 128), jnp.bfloat16),
         in_specs=[pl.BlockSpec(memory_space=pltpu.SMEM), vmem, vmem, vmem, vmem],
         out_specs=vmem,
-        scratch_shapes=[pltpu.VMEM((SEQ // BLOCKS, 64 * BLOCKS, 512), jnp.float32)],
-        compiler_params=pltpu.CompilerParams(vmem_limit_bytes=16 * MIB),
+        scratch_shapes=[pltpu.VMEM((SEQ // BLOCKS, 64 * BLOCKS, 512), jnp.float32)] * 2,
+        compiler_params=pltpu.CompilerParams(vmem_limit_bytes=24 * MIB),
         name="attend",
     )(ranges, kv, q, marks, seg)
 
@@ -561,6 +634,7 @@
     gain_ref,
     out_ref,
     landed,
+    units,
     w_out,
     w_proj,
     conv_w,
@@ -574,23 +648,38 @@
     own_sem,
 ):
     me = lax.axis_index("seq")
-    greet_all(me)
+    greet_row(me)
+    for there in (-1, 1):
+
+        @pl.when((me + there >= 0) & (me + there < SEQ))
+        def _():
+            greet(seq(lax.rem(me + SEQ + there, SEQ)))
+
     loads = [
         pltpu.make_async_copy(a, b, w_sem.at[i])
-        for i, (a, b) in enumerate(((w_out_ref, w_out), (w_proj_ref, w_proj), (w_ref, conv_w)))
+        for i, (a, b) in enumerate(
+            (
+                (units_ref, units),
+                (w_out_ref, w_out),
+                (w_proj_ref, w_proj),
+                (w_ref, conv_w),
+            )
+        )
     ]
     for load in loads:
         load.start()
-    await_all()
+    await_greetings(
+        CHIPS - 1 + jnp.where(me > 0, 1, 0) + jnp.where(me < SEQ - 1, 1, 0)
+    )
     send_back(o_ref, landed, o_send, o_recv, own_sem, me)
-    loads[0].wait()
-    loads[1].wait()
+    for load in loads[:3]:
+        load.wait()
 
     def base_of(device):
         return jnp.clip(device - 1, 0, SEQ - 3)
 
     base = base_of(me)
-    window[me - base] = project(landed, units_ref, w_out[...], w_proj[...])
+    window[me - base] = project(landed, units, w_out[...], w_proj[...])
 
     def near_copy(i, source, target):
         slot = source - base_of(target)
@@ -628,7 +717,7 @@
                 device_id_type=MESH,
             ).wait_recv()
 
-    loads[2].wait()
+    loads[3].wait()
     make_frames(
         me, base, base + 1, range_ref, window, start_ref, end_ref, conv_w, b_ref, gain_ref, out_ref, stacked
     )
@@ -646,11 +735,12 @@
     return pl.pallas_call(
         finish_near_kernel,
         out_shape=jax.ShapeDtypeStruct((FRAMES, CHANNELS), jnp.bfloat16),
-        in_specs=[pl.BlockSpec(memory_space=pltpu.SMEM), vmem, vmem, any_space, any_space]
+        in_specs=[pl.BlockSpec(memory_space=pltpu.SMEM), any_space, any_space, any_space, any_space]
         + [vmem, vmem, any_space, vmem, vmem],
         out_specs=vmem,
         scratch_shapes=[
             pltpu.VMEM((HEADS, HEAD, 128), jnp.bfloat16),
+            pltpu.VMEM((ROWS, WIDTH), jnp.bfloat16),
             pltpu.VMEM((WIDTH, WIDTH), jnp.bfloat16),
             pltpu.VMEM((WIDTH, CHANNELS), jnp.bfloat16),
             pltpu.VMEM((KERNEL * CHANNELS, CHANNELS), jnp.bfloat16),
@@ -660,7 +750,7 @@
             dma((CHIPS,)),
             dma((4,)),
             dma((3,)),
-            dma((3,)),
+            dma((4,)),
             dma,
         ],
         compiler_params=pltpu.CompilerParams(
@@ -675,7 +765,7 @@
 ):
     me = lax.axis_index("seq")
     greet_all(me)
-    await_all()
+    await_greetings(SEQ - 1)
     send_back(o_ref, landed, o_send, o_recv, own_sem, me)
     out_ref[...] = project(landed, units_ref, w_out_ref[...], w_proj_ref[...])
 
@@ -704,7 +794,7 @@
 def gather_kernel(block_ref, whole_ref, send_sem, recv_sem, own_sem):
     me = lax.axis_index("seq")
     greet_all(me)
-    await_all()
+    await_greetings(SEQ - 1)
 
     def copy(i, source):
         return pltpu.make_async_remote_copy(

time: 80.7 us -> 74 us (0.917)
  the two profiles are of different devices: /device:TPU:4 before, /device:TPU:1 now
where the time goes in v3:
time: 74 us; the launch traced here: 73.3 us
  Pallas kernels  66 us (89%)
  local copies, waits for them, and re-layouts  5.35 us (7%)
  other arithmetic  1.24 us (2%)
  between operations  0.76 us (1%)
    pallas_call x1, Pallas kernels, spread(): pl.pallas_call(spread_kernel, out_shape=(jax.ShapeDtypeStruct((SEQ, 2, RO...  34.7 us
    pallas_call x1, Pallas kernels, finish_near(): pl.pallas_call(finish_near_kernel, out_shape=jax.ShapeDtypeStruct((FRAMES...  24.2 us
    pallas_call x1, Pallas kernels, attend(): pl.pallas_call(attend_kernel, out_shape=jax.ShapeDtypeStruct((CHIPS, HEAD...  6.96 us
    unnamed x21, local copies, waits for them, and re-layouts  4.83 us

profile of v3, /device:TPU:1, one launch (start us, length us, event | category | flops | bytes accessed | tf_op | source)
XLA Modules:
  0.0 73.3 jit_solution(3135801937389010352)
XLA Ops:
  0.0 1.2 %pad_add_fusion.meta_ref = s32[2,128]{1,0:T(2,128)} fusion(s32[1,128]{1,0:T(1,128)} %bitcast.14, s32[1,128]{1,0:T(1,128)} %bitcast.15), kind=kLoop, calls=%fused_computation | loop fusion | flops 256 | bytes 2048 | tf_op jit(solution)/shard_map/stack | solution.py:876
  1.2 0.0 copy-start.6
  1.2 0.0 copy-start.7
  1.2 0.0 copy-start.8
  1.2 0.0 copy-start.9
  1.3 0.0 copy-start.10
  1.3 0.0 copy-start.11
  1.3 34.7 %spread.1 = (bf16[32,2,64,128]{3,2,1,0:T(8,128)(2,1)}, bf16[16,64,128]{2,1,0:T(8,128)(2,1)}, bf16[32,64,128]{2,1,0:T(8,128)(2,1)}, s32[32,128]{1,0:T(8,128)}, s3...) custom-call(bf16[128,1024]{1,0:T(8,128)(2,1)} %units_ref.1, f32[1,1024]{1,0:T(1,128)} %bitcast.13, ...), custom_call_target="tpu_custom_call" | custom-call | tf_op jit(solution)/shard_map/spread/pallas_call | solution.py:370
  36.0 0.5 slice.3
  37.2 0.0 copy-start.1
  37.2 1.2 %copy-done.1 = bf16[32,2,64,128]{3,2,1,0:T(8,128)(2,1)S(1)} copy-done((bf16[32,2,64,128]{3,2,1,0:T(8,128)(2,1)S(1)}, bf16[32,2,64,128]{3,2,1,0:T(8,128)(2,1)}, u32[]{:S(2)}) %copy-start.1) | copy-done | bytes 1048600
  38.4 0.0 copy-start.2
  38.4 1.0 %copy-done.2 = bf16[32,64,128]{2,1,0:T(8,128)(2,1)S(1)} copy-done((bf16[32,64,128]{2,1,0:T(8,128)(2,1)S(1)}, bf16[32,64,128]{2,1,0:T(8,128)(2,1)}, u32[]{:S(2)}) %copy-start.2) | copy-done | bytes 524312
  39.5 0.0 copy-start.4
  39.5 0.9 %copy-done.4 = bf16[16,64,128]{2,1,0:T(8,128)(2,1)S(1)} copy-done((bf16[16,64,128]{2,1,0:T(8,128)(2,1)S(1)}, bf16[16,64,128]{2,1,0:T(8,128)(2,1)}, u32[]{:S(2)}) %copy-start.4) | copy-done | bytes 262168
  40.4 0.0 copy-start.5
  40.4 0.7 copy-done.5
  41.1 7.0 %attend.1 = bf16[16,64,128]{2,1,0:T(8,128)(2,1)S(1)} custom-call(s32[48,128]{1,0:T(8,128)S(1)} %get-tuple-element.75.range_ref, bf16[32,2,64,128]{3,2,1,0:T(8,128)(2,1)S(1)} %copy-done.1, bf16[16,64,128]{2,1,0:T(8,128)(2,1)S(1)} %copy-done.4, bf16[32,64,128]{2,1,0:T(8,128)(2,1)S(1)} %copy-done.2, s32[32,128]{1,0:T(8,128)S(1)} %copy-done.5), custom_call_target="tpu_custom_call" | custom-call | tf_op jit(solution)/shard_map/attend/pallas_call | solution.py:532
  48.1 0.0 copy-done.6
  48.1 0.0 copy-done.7
  48.1 0.0 copy-done.8
  48.1 0.0 copy-done.9
  48.1 0.0 copy-done.10
  48.2 0.0 copy-done.11
  48.2 24.3 %conditional.1 = (bf16[768,512]{1,0:T(8,128)(2,1)S(1)}) conditional(s32[]{:T(128)} %bitcast.3, (bf16[16,64,128]{2,1,0:T(8,128)(2,1)S(1)}, bf16[128,1024]{1,0:T(8,128)(2,1)S(1)}, bf16[1024,1024]{1,0:T(8,128)(2,1)S(1)}, bf16[1024,512]{1,0:T(8,128)(2,1)S(1)}, s32[48,128]{1,0:T(8,128)S(1)}, /*index=5*/s32[32,128]{1,0:T(8,128)S(1)}, ...), branch_computations={%region_0.0_spmd, %region_1.0_spmd} | conditional | bytes 17301568 | solution.py:881
  48.2 24.2 %finish_near.1 = bf16[768,512]{1,0:T(8,128)(2,1)S(1)} custom-call(s32[48,128]{1,0:T(8,128)S(1)} %get-tuple-element.58.range_ref, bf16[16,64,128]{2,1,0:T(8,128)(2,1)S(1)} %get-tuple-element.59.o_ref, bf16[128,1024]{1,0:T(8,128)(2,1)S(1)} %get-tuple-element.60.units_ref, bf16[1024,1024]{1,0:T(8,128)(2,1)S(1)} %get-tuple-element.61.w_out_ref, ...), custom_call_target="tpu_custom_call" | custom-call | tf_op jit(solution)/shard_map/cond/branch_1_fun/finish_near/pallas_call | solution.py:735
  72.4 0.9 %copy.16 = bf16[768,512]{1,0:T(8,128)(2,1)} copy(bf16[768,512]{1,0:T(8,128)(2,1)S(1)} %get-tuple-element.82) | data formatting | bytes 1572864
Async XLA Ops:
  1.2 46.9 %copy-start.6 = (bf16[5,512,512]{2,1,0:T(8,128)(2,1)S(1)}, bf16[5,512,512]{2,1,0:T(8,128)(2,1)}, u32[]{:S(2)}) copy-start(bf16[5,512,512]{2,1,0:T(8,128)(2,1)} %param.19) | copy-start | bytes 7864324
  1.2 46.9 %copy-start.7 = (bf16[1024,1024]{1,0:T(8,128)(2,1)S(1)}, bf16[1024,1024]{1,0:T(8,128)(2,1)}, u32[]{:S(2)}) copy-start(bf16[1024,1024]{1,0:T(8,128)(2,1)} %param.17) | copy-start | bytes 6291460
  1.2 46.9 %copy-start.8 = (bf16[1024,512]{1,0:T(8,128)(2,1)S(1)}, bf16[1024,512]{1,0:T(8,128)(2,1)}, u32[]{:S(2)}) copy-start(bf16[1024,512]{1,0:T(8,128)(2,1)} %param.18) | copy-start | bytes 3145732
  1.2 46.9 %copy-start.9 = (bf16[128,1024]{1,0:T(8,128)(2,1)S(1)}, bf16[128,1024]{1,0:T(8,128)(2,1)}, u32[]{:S(2)}) copy-start(bf16[128,1024]{1,0:T(8,128)(2,1)} %units_ref.1) | copy-start | bytes 786436
  1.3 46.9 %copy-start.10 = (f32[512]{0:T(512)S(1)}, f32[512]{0:T(512)}, u32[]{:S(2)}) copy-start(f32[512]{0:T(512)} %param.20) | copy-start | bytes 6148
  1.3 46.9 %copy-start.11 = (f32[512]{0:T(512)S(1)}, f32[512]{0:T(512)}, u32[]{:S(2)}) copy-start(f32[512]{0:T(512)} %param.21) | copy-start | bytes 6148
  37.2 1.2 %copy-start.1 = (bf16[32,2,64,128]{3,2,1,0:T(8,128)(2,1)S(1)}, bf16[32,2,64,128]{3,2,1,0:T(8,128)(2,1)}, u32[]{:S(2)}) copy-start(bf16[32,2,64,128]{3,2,1,0:T(8,128)(2,1)} %get-tuple-element.76.kv_ref) | copy-start | bytes 3145732
  38.4 1.0 %copy-start.2 = (bf16[32,64,128]{2,1,0:T(8,128)(2,1)S(1)}, bf16[32,64,128]{2,1,0:T(8,128)(2,1)}, u32[]{:S(2)}) copy-start(bf16[32,64,128]{2,1,0:T(8,128)(2,1)} %get-tuple-element.78.mark_ref) | copy-start | bytes 1572868
  39.5 0.9 %copy-start.4 = (bf16[16,64,128]{2,1,0:T(8,128)(2,1)S(1)}, bf16[16,64,128]{2,1,0:T(8,128)(2,1)}, u32[]{:S(2)}) copy-start(bf16[16,64,128]{2,1,0:T(8,128)(2,1)} %get-tuple-element.77.q_ref) | copy-start | bytes 786436
  40.4 0.7 copy-start.5

commit v4 on v3

v4 whole, which is shorter than its diff:
```python
import functools

import jax
import jax.numpy as jnp
from jax import lax
from jax.experimental import pallas as pl
from jax.experimental.pallas import tpu as pltpu
from jax.sharding import PartitionSpec as P

MESH = pl.DeviceIdType.MESH
SEQ = 32
CHIPS = 16
HEADS = 16
HEAD = 64
ROWS = 128
WIDTH = 1024
UNITS = 4096
CHANNELS = 512
KERNEL = 5
FRAMES = 768
STEP = 96
STEPS = FRAMES // STEP
TILE = 256
BLOCKS = 8
GROUPS = 8
NEG = -1e30
MIB = 1024 * 1024


def seq(index):
    return {"seq": index}


def greet(device):
    pl.semaphore_signal(
        pltpu.get_barrier_semaphore(), 1, device_id=device, device_id_type=MESH
    )


def greet_all(me):
    def one(i, carry):
        greet(seq(lax.rem(me + i, SEQ)))
        return carry

    lax.fori_loop(1, SEQ, one, 0)


def greet_row(me):
    def one(i, carry):
        greet(seq(lax.rem(me + 2 * i, SEQ)))
        return carry

    lax.fori_loop(1, CHIPS, one, 0)


def await_greetings(count):
    pl.semaphore_wait(pltpu.get_barrier_semaphore(), count)


def group_at(own, i):
    flip = own + 1 - 2 * lax.rem(own, 2)
    if i == 0:
        return flip
    if i == 1:
        return lax.rem(flip + 2, 4)
    if i == 2:
        return lax.rem(own + 2, 4)
    return own


def base_of(device):
    return jnp.clip(device - 1, 0, SEQ - 3)


def low_lanes(rows):
    return lax.broadcasted_iota(jnp.int32, (rows, 128), 1) < HEAD


def mix_kernel(
    units_ref,
    gain_ref,
    own_seg_ref,
    own_dur_ref,
    w_ref,
    w_out_ref,
    w_proj_ref,
    window_ref,
    start_ref,
    end_ref,
    range_ref,
    far_ref,
    h_ref,
    meta_ref,
    wbuf,
    send_kv,
    send_q,
    meta_all,
    flags,
    kv_ref,
    q_ref,
    mark_ref,
    seg_ref,
    even_ref,
    odd_ref,
    send_o,
    landed,
    w_out,
    w_proj,
    mine,
    w_sem,
    load_sem,
    kv_send,
    kv_recv,
    q_send,
    q_recv,
    pass_send,
    pass_recv,
    meta_send,
    meta_recv,
    flag_send,
    flag_recv,
    o_send,
    o_recv,
    near_send,
    near_recv,
    own_sem,
):
    me = lax.axis_index("seq")
    part = lax.axis_index("grp")
    core = lax.rem(me, 2)
    chip = me // 2
    sibling = me + 1 - 2 * core
    own = chip // 4
    greet_row(me)
    for there in (-1, 1):

        @pl.when((me + there >= 0) & (me + there < SEQ))
        def _():
            greet(seq(lax.rem(me + SEQ + there, SEQ)))

    def greet_part(i, carry):
        greet({"grp": lax.rem(part + i, GROUPS)})
        return carry

    lax.fori_loop(1, GROUPS, greet_part, 0)

    def w_copy(i, t):
        g = group_at(own, i)
        return pltpu.make_async_copy(
            w_ref.at[:, pl.ds(t * WIDTH + g * 256, 256)], wbuf.at[i, t], w_sem.at[i, t]
        )

    for i in range(4):
        w_copy(i, 1).start()
        w_copy(i, 2).start()
    for i in range(4):
        w_copy(i, 0).start()
    loads = [
        pltpu.make_async_copy(a, b, load_sem.at[i])
        for i, (a, b) in enumerate(((w_out_ref, w_out), (w_proj_ref, w_proj)))
    ]
    for load in loads:
        load.start()

    meta_ref[0:1, :] = own_seg_ref[...]
    meta_ref[1:2, :] = own_dur_ref[...]
    x = units_ref[...].astype(jnp.float32)
    mean = jnp.mean(x, axis=-1, keepdims=True)
    centred = x - mean
    variance = jnp.mean(centred * centred, axis=-1, keepdims=True)
    h_ref[...] = (centred / jnp.sqrt(variance + 1e-05) * gain_ref[...]).astype(jnp.bfloat16)

    def meta_copy(i, source):
        return pltpu.make_async_remote_copy(
            src_ref=meta_ref,
            dst_ref=meta_all.at[source, core],
            send_sem=meta_send.at[i],
            recv_sem=meta_recv.at[source],
            device_id=seq(lax.rem(me + 2 * i, SEQ)),
            device_id_type=MESH,
        )

    def send_meta(i, carry):
        meta_copy(i, chip).start()
        return carry

    own_meta = pltpu.make_async_copy(meta_ref, meta_all.at[chip, core], own_sem.at[2])
    pass_meta = pltpu.make_async_remote_copy(
        src_ref=meta_all.at[:, core],
        dst_ref=meta_all.at[:, core],
        send_sem=meta_send.at[0],
        recv_sem=own_sem.at[3],
        device_id=seq(sibling),
        device_id_type=MESH,
    )

    def kv_copy(head, source):
        return pltpu.make_async_remote_copy(
            src_ref=send_kv.at[head],
            dst_ref=kv_ref.at[2 * source + core],
            send_sem=kv_send.at[head],
            recv_sem=kv_recv.at[source],
            device_id=seq(2 * head + core),
            device_id_type=MESH,
        )

    def q_copy(head, source):
        return pltpu.make_async_remote_copy(
            src_ref=send_q.at[head],
            dst_ref=q_ref.at[source],
            send_sem=q_send.at[head],
            recv_sem=q_recv.at[source],
            device_id=seq(2 * head + core),
            device_id_type=MESH,
        )

    own_kv = pltpu.make_async_copy(send_kv.at[chip], kv_ref.at[me], own_sem.at[0])
    own_q = pltpu.make_async_copy(send_q.at[chip], q_ref.at[chip], own_sem.at[1])
    own_pass = pltpu.make_async_remote_copy(
        src_ref=send_kv.at[chip],
        dst_ref=kv_ref.at[me],
        send_sem=pass_send.at[chip],
        recv_sem=pass_recv.at[chip],
        device_id=seq(sibling),
        device_id_type=MESH,
    )

    low = low_lanes(ROWS // 2)
    for i in range(4):
        g = group_at(own, i)
        w_copy(i, 1).wait()
        w_copy(i, 2).wait()
        h = h_ref[...]
        k4, v4 = (
            jnp.dot(h, wbuf[i, t], preferred_element_type=jnp.float32) for t in (1, 2)
        )
        for j in range(2):
            at = slice(128 * j, 128 * j + 128)
            v2 = jnp.transpose(v4[:, at]).astype(jnp.bfloat16)
            k2 = k4[:, at]
            turned = pltpu.roll(k2, HEAD, 1)
            first = 4 * g + 2 * j
            send_kv[first, 0] = jnp.where(low, k2[:64], turned[64:]).astype(jnp.bfloat16)
            send_kv[first + 1, 0] = jnp.where(low, turned[:64], k2[64:]).astype(jnp.bfloat16)
            send_kv[first, 1] = v2[:64]
            send_kv[first + 1, 1] = v2[64:]
        if i == 0:
            beside = jnp.where(me > 0, 1, 0) + jnp.where(me < SEQ - 1, 1, 0)
            await_greetings(CHIPS - 1 + beside + GROUPS - 1)
        for r in range(4):
            if i == 3 and r == 0:
                own_kv.start()
                own_pass.start()
            else:
                kv_copy(4 * g + lax.rem(chip + r, 4), chip).start()
        if i == 0:
            lax.fori_loop(1, CHIPS, send_meta, 0)
            own_meta.start()
    for i in range(4):
        g = group_at(own, i)
        w_copy(i, 0).wait()
        q4 = jnp.dot(h_ref[...], wbuf[i, 0], preferred_element_type=jnp.float32) * 0.125
        for j in range(2):
            q2 = jnp.transpose(q4[:, 128 * j : 128 * j + 128]).astype(jnp.bfloat16)
            first = 4 * g + 2 * j
            send_q[first] = q2[:64]
            send_q[first + 1] = q2[64:]
        for r in range(4):
            if i == 3 and r == 0:
                own_q.start()
            else:
                q_copy(4 * g + lax.rem(chip + r, 4), chip).start()

    def await_meta(i, carry):
        meta_copy(i, lax.rem(chip + CHIPS - i, CHIPS)).wait()
        return carry

    lax.fori_loop(1, CHIPS, await_meta, 0)
    own_meta.wait()
    pass_meta.start()
    pass_meta.wait()
    meta = meta_all[...].reshape(SEQ, 2, 128)

    seg = meta[:, 0, :]
    dur = meta[:, 1, :].astype(jnp.float32)
    lower = (
        lax.broadcasted_iota(jnp.int32, (128, 128), 0)
        <= lax.broadcasted_iota(jnp.int32, (128, 128), 1)
    ).astype(jnp.float32).astype(jnp.bfloat16)
    earlier = (
        lax.broadcasted_iota(jnp.int32, (SEQ, SEQ), 0)
        > lax.broadcasted_iota(jnp.int32, (SEQ, SEQ), 1)
    ).astype(jnp.float32).astype(jnp.bfloat16)
    dur16 = dur.astype(jnp.bfloat16)
    within = jnp.dot(dur16, lower, preferred_element_type=jnp.float32)
    before = jnp.dot(earlier, dur16, preferred_element_type=jnp.float32)
    ends = within + jnp.sum(before, axis=1, keepdims=True)
    seg_ref[...] = seg
    start_ref[...] = (ends - dur).astype(jnp.int32)
    end_ref[...] = ends.astype(jnp.int32)

    first_frame = start_ref[:, 0:1]
    index = lax.broadcasted_iota(jnp.int32, (SEQ, 1), 0)
    late = (index >= 1) & (index <= SEQ - 3) & (first_frame > FRAMES * (index + 1) - 2)
    early = (index >= 3) & (first_frame < FRAMES * (index - 2) + FRAMES + 2)
    far = jnp.sum(jnp.where(late | early, 1.0, 0.0))
    flags[part] = jnp.zeros((8, 128), jnp.float32) + far

    def flag_copy(i, source):
        return pltpu.make_async_remote_copy(
            src_ref=flags.at[source],
            dst_ref=flags.at[source],
            send_sem=flag_send.at[i],
            recv_sem=flag_recv.at[source],
            device_id={"grp": lax.rem(part + i, GROUPS)},
            device_id_type=MESH,
        )

    def send_flag(i, carry):
        flag_copy(i, part).start()
        return carry

    lax.fori_loop(1, GROUPS, send_flag, 0)

    lane8 = lax.broadcasted_iota(jnp.int32, (8, 128), 1)
    block = jnp.zeros((8, 128), jnp.int32)
    for f in range(STEPS):
        t0 = (FRAMES * me + STEP * f - KERNEL // 2).astype(jnp.float32)
        passed = jnp.sum((ends <= t0).astype(jnp.float32)).astype(jnp.int32)
        block = jnp.where(lane8 == f, passed, block)
    range_ref[...] = block

    def mark(b, carry):
        row = jnp.broadcast_to(seg_ref[pl.ds(b, 1), :].astype(jnp.float32), (128, 128))
        column = jnp.transpose(row)
        place = lax.broadcasted_iota(jnp.int32, (64, 128), 1).astype(jnp.float32)
        marked = jnp.where(
            place < 8.0,
            jnp.where(place == column[:64], 1.0, 0.0),
            jnp.where(place == column[64:] + 8.0, 1.0, 0.0),
        )
        mark_ref[b] = marked.astype(jnp.bfloat16)
        return carry

    lax.fori_loop(0, SEQ, mark, 0)

    def await_flag(i, carry):
        flag_copy(i, lax.rem(part + GROUPS - i, GROUPS)).wait_recv()
        flag_copy(i, part).wait_send()
        return carry

    lax.fori_loop(1, GROUPS, await_flag, 0)
    total = flags[0]
    for i in range(1, GROUPS):
        total = total + flags[i]
    far_ref[0, 0] = jnp.sum(total).astype(jnp.int32)

    def passing(source):
        return pltpu.make_async_remote_copy(
            src_ref=kv_ref.at[2 * source + core],
            dst_ref=kv_ref.at[2 * source + core],
            send_sem=pass_send.at[source],
            recv_sem=pass_recv.at[source],
            device_id=seq(sibling),
            device_id_type=MESH,
        )

    for i in range(4):
        for r in range(4):
            if i == 3 and r == 0:
                continue
            source = 4 * group_at(own, i) + lax.rem(chip + 4 - r, 4)
            kv_copy(source, source).wait_recv()
            passing(source).start()

    for i in range(4):
        for r in range(4):
            source = 4 * group_at(own, i) + lax.rem(chip + 4 - r, 4)
            if i == 3 and r == 0:
                own_kv.wait()
                own_q.wait()
                own_pass.wait_recv()
            else:
                q_copy(source, source).wait_recv()
                passing(source).wait_recv()

    pairs = CHIPS // 2

    def pair_at(i):
        return lax.rem(chip // 2 + i, pairs)

    ones = jnp.ones((16, 128 * BLOCKS), jnp.bfloat16)

    def right_side(p):
        first = 4 * p + core
        q = jnp.concatenate([q_ref[2 * p], q_ref[2 * p + 1]], axis=1)
        zero = jnp.zeros((HEAD, 256), jnp.bfloat16)
        rows = lax.broadcasted_iota(jnp.int32, (8, 128), 0)
        bias = jnp.concatenate(
            [
                jnp.where(seg_ref[pl.ds(first + 2 * e, 1), :] == rows, 0.0, NEG)
                for e in range(2)
            ],
            axis=1,
        )
        none = jnp.zeros((8, 256), jnp.float32)
        biases = jnp.concatenate(
            [jnp.concatenate([bias, none], axis=0), jnp.concatenate([none, bias], axis=0)],
            axis=1,
        ).astype(jnp.bfloat16)
        return jnp.concatenate(
            [
                jnp.concatenate([q, zero], axis=1),
                jnp.concatenate([zero, q], axis=1),
                biases,
                jnp.zeros((112, 512), jnp.bfloat16),
            ],
            axis=0,
        )

    def score(right, block, keep, top):
        left = jnp.concatenate(
            [
                jnp.concatenate([kv_ref[block + t, 0], mark_ref[block + t]], axis=1)
                for t in range(BLOCKS)
            ],
            axis=0,
        )
        s = jnp.dot(left, right, preferred_element_type=jnp.float32)
        keep[...] = s
        return jnp.maximum(top, jnp.max(s.reshape(8 * BLOCKS, 8, 512), axis=0))

    def collect(top, block, kept, acc):
        w = jnp.exp(kept[...] - top).astype(jnp.bfloat16)
        w = jnp.concatenate(
            [
                w[64 * t : 64 * t + 64, 256 * h : 256 * h + 256]
                for t in range(BLOCKS)
                for h in range(2)
            ],
            axis=0,
        )
        v = jnp.concatenate([kv_ref[block + t, 1] for t in range(BLOCKS)], axis=1)
        v = jnp.concatenate([v, ones], axis=0)
        return acc + jnp.dot(v, w, preferred_element_type=jnp.float32)

    def peak(top):
        top = jnp.max(jnp.maximum(top[:, :256], top[:, 256:]), axis=0, keepdims=True)
        return jnp.concatenate([top, top], axis=1)

    def o_copy(target, source):
        return pltpu.make_async_remote_copy(
            src_ref=send_o.at[target],
            dst_ref=landed.at[source],
            send_sem=o_send.at[target],
            recv_sem=o_recv.at[source],
            device_id=seq(2 * target + core),
            device_id_type=MESH,
        )

    own_o = pltpu.make_async_copy(send_o.at[chip], landed.at[chip], own_sem.at[4])

    def give(i, acc):
        p = pair_at(i)
        out = (acc[:HEAD] / acc[HEAD : HEAD + 1]).astype(jnp.bfloat16)
        send_o[2 * p] = out[:, :128]
        send_o[2 * p + 1] = out[:, 128:]
        for e in range(2):

            @pl.when(2 * p + e != chip)
            def _():
                o_copy(2 * p + e, chip).start()

            @pl.when(2 * p + e == chip)
            def _():
                own_o.start()

    low = jnp.full((8, 512), NEG, jnp.float32)
    clear = jnp.zeros((HEAD + 16, 256), jnp.float32)
    chunks = SEQ // BLOCKS
    right = right_side(pair_at(0))
    top = low
    for n in range(chunks):
        top = score(right, BLOCKS * n, even_ref.at[n], top)

    def both(i, here, there, top):
        right = right_side(pair_at(i))
        new_top, acc = low, clear
        for n in range(chunks):
            new_top = score(right, BLOCKS * n, here.at[n], new_top)
            acc = collect(top, BLOCKS * n, there.at[n], acc)
        give(i - 1, acc)
        return peak(new_top)

    def two(i, top):
        top = both(2 * i + 1, odd_ref, even_ref, top)
        return both(2 * i + 2, even_ref, odd_ref, top)

    top = lax.fori_loop(0, pairs // 2 - 1, two, peak(top))
    top = both(pairs - 1, odd_ref, even_ref, top)
    acc = clear
    for n in range(chunks):
        acc = collect(top, BLOCKS * n, odd_ref.at[n], acc)
    give(pairs - 1, acc)

    for load in loads:
        load.wait()

    def receive(i, carry):
        o_copy(chip, lax.rem(chip + CHIPS - i, CHIPS)).wait_recv()
        return carry

    own_o.wait()
    lax.fori_loop(1, CHIPS, receive, 0)
    turned = [
        jnp.transpose(
            jnp.concatenate([landed[2 * j], landed[2 * j + 1]], axis=0).astype(jnp.float32)
        ).astype(jnp.bfloat16)
        for j in range(HEADS // 2)
    ]
    attended = jnp.concatenate(turned, axis=1)
    mixed = jnp.dot(attended, w_out[...], preferred_element_type=jnp.float32)
    mixed = (mixed + units_ref[...].astype(jnp.float32)).astype(jnp.bfloat16)
    mine[...] = jnp.dot(mixed, w_proj[...], preferred_element_type=jnp.float32).astype(
        jnp.bfloat16
    )

    def near_copy(i, target):
        slot = me - base_of(target)
        return pltpu.make_async_remote_copy(
            src_ref=mine,
            dst_ref=window_ref.at[slot],
            send_sem=near_send.at[i],
            recv_sem=near_recv.at[slot],
            device_id=seq(target),
            device_id_type=MESH,
        )

    routes = (
        (me > 0, lax.rem(me + SEQ - 1, SEQ)),
        (me < SEQ - 1, lax.rem(me + 1, SEQ)),
        (me == 2, 0),
        (me == SEQ - 3, SEQ - 1),
    )
    for i, (present, target) in enumerate(routes):

        @pl.when(present)
        def _():
            near_copy(i, target).start()

    base = base_of(me)
    own_window = pltpu.make_async_copy(mine, window_ref.at[me - base], own_sem.at[5])
    own_window.start()

    def sent(i, carry):
        o_copy(lax.rem(chip + i, CHIPS), chip).wait_send()
        return carry

    lax.fori_loop(1, CHIPS, sent, 0)
    for i in range(4):
        for r in range(4):
            source = 4 * group_at(own, i) + lax.rem(chip + 4 - r, 4)
            if i < 3 or r > 0:
                q_copy(source, source).wait_send()
                kv_copy(source, source).wait_send()
                passing(source).wait_send()
    own_pass.wait_send()

    for slot in range(3):

        @pl.when(slot != me - base)
        def _():
            pltpu.make_async_remote_copy(
                src_ref=mine,
                dst_ref=window_ref.at[slot],
                send_sem=near_send.at[0],
                recv_sem=near_recv.at[slot],
                device_id=seq(sibling),
                device_id_type=MESH,
            ).wait_recv()

    for i, (present, target) in enumerate(routes):

        @pl.when(present)
        def _():
            near_copy(i, target).wait_send()

    own_window.wait()


def mix(units, gain, seg, dur, w_qkv, w_out, w_proj):
    any_space = pl.BlockSpec(memory_space=pl.ANY)
    vmem = pl.BlockSpec(memory_space=pltpu.VMEM)
    dma = pltpu.SemaphoreType.DMA
    half = (ROWS // 2, 128)
    return pl.pallas_call(
        mix_kernel,
        out_shape=(
            jax.ShapeDtypeStruct((3, ROWS, CHANNELS), jnp.bfloat16),
            jax.ShapeDtypeStruct((SEQ, 128), jnp.int32),
            jax.ShapeDtypeStruct((SEQ, 128), jnp.int32),
            jax.ShapeDtypeStruct((8, 128), jnp.int32),
            jax.ShapeDtypeStruct((1, 1), jnp.int32),
        ),
        in_specs=[vmem] * 4 + [any_space] * 3,
        out_specs=(any_space, vmem, vmem, vmem, pl.BlockSpec(memory_space=pltpu.SMEM)),
        scratch_shapes=[
            pltpu.VMEM((ROWS, WIDTH), jnp.bfloat16),
            pltpu.VMEM((2, 128), jnp.int32),
            pltpu.VMEM((4, 3, WIDTH, 256), jnp.bfloat16),
            pltpu.VMEM((HEADS, 2) + half, jnp.bfloat16),
            pltpu.VMEM((HEADS,) + half, jnp.bfloat16),
            pltpu.VMEM((CHIPS, 2, 2, 128), jnp.int32),
            pltpu.VMEM((GROUPS, 8, 128), jnp.float32),
            pltpu.VMEM((SEQ, 2) + half, jnp.bfloat16),
            pltpu.VMEM((CHIPS,) + half, jnp.bfloat16),
            pltpu.VMEM((SEQ,) + half, jnp.bfloat16),
            pltpu.VMEM((SEQ, 128), jnp.int32),
            pltpu.VMEM((SEQ // BLOCKS, 64 * BLOCKS, 512), jnp.float32),
            pltpu.VMEM((SEQ // BLOCKS, 64 * BLOCKS, 512), jnp.float32),
            pltpu.VMEM((CHIPS,) + half, jnp.bfloat16),
            pltpu.VMEM((CHIPS,) + half, jnp.bfloat16),
            pltpu.VMEM((WIDTH, WIDTH), jnp.bfloat16),
            pltpu.VMEM((WIDTH, CHANNELS), jnp.bfloat16),
            pltpu.VMEM((ROWS, CHANNELS), jnp.bfloat16),
            dma((4, 3)),
            dma((2,)),
            dma((HEADS,)),
            dma((HEADS,)),
            dma((HEADS,)),
            dma((HEADS,)),
            dma((HEADS,)),
            dma((HEADS,)),
            dma((CHIPS,)),
            dma((CHIPS,)),
            dma((GROUPS,)),
            dma((GROUPS,)),
            dma((CHIPS,)),
            dma((CHIPS,)),
            dma((4,)),
            dma((3,)),
            dma((6,)),
        ],
        compiler_params=pltpu.CompilerParams(
            collective_id=1, has_side_effects=True, vmem_limit_bytes=56 * MIB
        ),
        name="mix",
    )(units, gain, seg, dur, w_qkv, w_out, w_proj)


def make_frames(
    me, base, last, range_ref, window_ref, start_ref, end_ref, w_ref, b_ref, gain_ref, out_ref, stacked
):
    for f in range(STEPS):
        block = jnp.clip(range_ref[0, f] // 128, base, last)
        starts = jnp.concatenate(
            [start_ref[pl.ds(block, 1), :], start_ref[pl.ds(block + 1, 1), :]], axis=1
        )
        ends = jnp.concatenate(
            [end_ref[pl.ds(block, 1), :], end_ref[pl.ds(block + 1, 1), :]], axis=1
        )
        window = window_ref[pl.ds(block - base, 2)].reshape(256, CHANNELS)
        frame = lax.broadcasted_iota(jnp.int32, (STEP, 256), 0)
        first = FRAMES * me + STEP * f - KERNEL // 2
        starts, ends = starts - first, ends - first
        for j in range(KERNEL):
            chosen = jnp.where((frame >= starts - j) & (frame < ends - j), 1.0, 0.0)
            rows = jnp.dot(
                chosen.astype(jnp.bfloat16), window, preferred_element_type=jnp.float32
            )
            stacked[STEP * f : STEP * f + STEP, CHANNELS * j : CHANNELS * j + CHANNELS] = (
                rows.astype(jnp.bfloat16)
            )
    bias, gain = b_ref[...], gain_ref[...]
    for r in range(FRAMES // TILE):
        at = slice(TILE * r, TILE * r + TILE)
        conv = jnp.dot(stacked[at, :], w_ref[...], preferred_element_type=jnp.float32) + bias
        value = jnp.maximum(conv, 0.0)
        mean = jnp.mean(value, axis=-1, keepdims=True)
        centred = value - mean
        variance = jnp.mean(centred * centred, axis=-1, keepdims=True)
        half = KERNEL // 2
        centre = stacked[at, half * CHANNELS : (half + 1) * CHANNELS].astype(jnp.float32)
        result = centre + centred / jnp.sqrt(variance + 1e-05) * gain
        out_ref[at, :] = result.astype(jnp.bfloat16)


def gather_kernel(block_ref, whole_ref, send_sem, recv_sem, own_sem):
    me = lax.axis_index("seq")
    greet_all(me)
    await_greetings(SEQ - 1)

    def copy(i, source):
        return pltpu.make_async_remote_copy(
            src_ref=block_ref,
            dst_ref=whole_ref.at[source],
            send_sem=send_sem.at[i],
            recv_sem=recv_sem.at[source],
            device_id=seq(lax.rem(me + i, SEQ)),
            device_id_type=MESH,
        )

    def send(i, carry):
        copy(i, me).start()
        return carry

    def receive(i, carry):
        copy(i, lax.rem(me + SEQ - i, SEQ)).wait()
        return carry

    lax.fori_loop(1, SEQ, send, 0)
    own = pltpu.make_async_copy(block_ref, whole_ref.at[me], own_sem)
    own.start()
    lax.fori_loop(1, SEQ, receive, 0)
    own.wait()


def gather(reduced):
    any_space = pl.BlockSpec(memory_space=pl.ANY)
    dma = pltpu.SemaphoreType.DMA
    return pl.pallas_call(
        gather_kernel,
        out_shape=jax.ShapeDtypeStruct((SEQ, ROWS, CHANNELS), jnp.bfloat16),
        in_specs=[any_space],
        out_specs=any_space,
        scratch_shapes=[dma((SEQ,)), dma((SEQ,)), dma],
        compiler_params=pltpu.CompilerParams(collective_id=4, has_side_effects=True),
        name="gather",
    )(reduced)


def frames_kernel(
    near, range_ref, rows_ref, start_ref, end_ref, w_ref, b_ref, gain_ref, out_ref, stacked
):
    me = lax.axis_index("seq")
    base = base_of(me) if near else 0
    last = base + 1 if near else SEQ - 2
    make_frames(
        me, base, last, range_ref, rows_ref, start_ref, end_ref, w_ref, b_ref, gain_ref, out_ref, stacked
    )


def frames(near, ranges, rows, starts, ends, conv_w, conv_b, conv_gain):
    vmem = pl.BlockSpec(memory_space=pltpu.VMEM)
    return pl.pallas_call(
        functools.partial(frames_kernel, near),
        out_shape=jax.ShapeDtypeStruct((FRAMES, CHANNELS), jnp.bfloat16),
        in_specs=[pl.BlockSpec(memory_space=pltpu.SMEM)] + [vmem] * 6,
        out_specs=vmem,
        scratch_shapes=[pltpu.VMEM((FRAMES, KERNEL * CHANNELS), jnp.bfloat16)],
        compiler_params=pltpu.CompilerParams(vmem_limit_bytes=60 * MIB),
        name="frames_near" if near else "frames_far",
    )(ranges, rows, starts, ends, conv_w, conv_b, conv_gain)


def finish_near(ranges, window, *rest):
    return frames(True, ranges, window, *rest)


def finish_far(ranges, window, *rest):
    me = lax.axis_index("seq")
    own = lax.dynamic_index_in_dim(window, me - base_of(me), 0, keepdims=False)
    return frames(False, ranges, gather(own), *rest)


def local(units, durations, seg_ids, ln_gain, w_qkv, w_out, w_proj, conv_w, conv_b, conv_gain):
    window, starts, ends, ranges, far = mix(
        units,
        ln_gain.reshape(1, WIDTH),
        seg_ids.reshape(1, ROWS),
        durations.reshape(1, ROWS),
        w_qkv,
        w_out,
        w_proj,
    )
    return lax.cond(
        far.reshape(()) == 0,
        finish_near,
        finish_far,
        ranges,
        window,
        starts,
        ends,
        conv_w.reshape(KERNEL * CHANNELS, CHANNELS),
        conv_b.reshape(1, CHANNELS),
        conv_gain.reshape(1, CHANNELS),
    )


def solution(mesh):
    parted = P(("grp", "seq"))
    wide = P(("grp", "seq"), None)
    return jax.shard_map(
        local,
        mesh=mesh,
        in_specs=(wide, parted, parted) + (P(),) * 7,
        out_specs=wide,
        check_vma=False,
    )
```

time: 74 us -> 60.7 us (0.82)
  Pallas kernels: 66 us -> 58.1 us
  local copies, waits for them, and re-layouts: 5.35 us -> 0.89 us
  other arithmetic: 1.24 us -> 0 us
    pallas_call x3 -> x2, Pallas kernels: 66 us -> 58.1 us  [the longest x1 52.9 us: mix(): pl.pallas_call(mix_kernel, out_shape=(jax.ShapeDtypeStruct((3, ROWS, CHAN...]
    unnamed x21 -> x8, local copies, waits for them, and re-layouts: 4.83 us -> 0.89 us
    another operation x1 -> x0, other arithmetic: 1.24 us -> none  [local(): meta = jnp.stack([seg_ids, durations])]
where the time goes in v4:
time: 60.7 us; the launch traced here: 59.8 us
  Pallas kernels  58.1 us (96%)
  local copies, waits for them, and re-layouts  0.89 us (1%)
  between operations  0.61 us (1%)
    pallas_call x1, Pallas kernels, mix(): pl.pallas_call(mix_kernel, out_shape=(jax.ShapeDtypeStruct((3, ROWS, CHAN...  52.9 us
    pallas_call x1, Pallas kernels, frames(): pl.pallas_call(functools.partial(frames_kernel, near), out_shape=jax.Shap...  5.15 us

profile of v4, /device:TPU:1, one launch (start us, length us, event | category | flops | bytes accessed | tf_op | source)
XLA Modules:
  0.0 59.8 jit_solution(13774095767684763678)
XLA Ops:
  0.0 0.0 copy-start
  0.0 0.0 copy-start.2
  0.0 0.0 copy-start.3
  0.0 52.9 %mix.1 = (bf16[3,128,512]{2,1,0:T(8,128)(2,1)}, s32[32,128]{1,0:T(8,128)S(1)}, s32[32,128]{1,0:T(8,128)S(1)}, s32[8,128]{1,0:T(8,128)S(1)}, s32[1,1]{1,0:T(1,128)}) custom-call(bf16[128,1024]{1,0:T(8,128)(2,1)} %units_ref.1, f32[1,1024]{1,0:T(1,128)} %bitcast.15, s32[1,128]{1,0:T(1,128)} %bitcast.16, s32[1,128]{1,0:T(1,128)} %bitcast.17, ...), custom_call_target="tpu_custom_call" | custom-call | tf_op jit(solution)/shard_map/mix/pallas_call | solution.py:596
  53.5 0.0 copy-done
  53.5 0.0 copy-done.2
  53.5 0.0 copy-done.3
  53.5 5.3 %conditional.1 = (bf16[768,512]{1,0:T(8,128)(2,1)S(1)}) conditional(s32[]{:T(128)} %bitcast.4, (bf16[3,128,512]{2,1,0:T(8,128)(2,1)}, s32[8,128]{1,0:T(8,128)S(1)}, s32[32,128]{1,0:T(8,128)S(1)}, s32[32,128]{1,0:T(8,128)S(1)}, bf16[2560,512]{1,0:T(8,128)(2,1)S(1)}, /*index=5*/f32[1,512]{1,0:T(1,128)S(1)}, f32[1,512]{1,0:T(1,128)S(1)}) %tuple.22, ...), branch_computations={%region_0.1_spmd, %region_1.2_spmd} | conditional | flops 10 | bytes 262270 | solution.py:776
  53.7 5.2 %frames_near.1 = bf16[768,512]{1,0:T(8,128)(2,1)S(1)} custom-call(s32[8,128]{1,0:T(8,128)S(1)} %get-tuple-element.43.range_ref, bf16[3,128,512]{2,1,0:T(8,128)(2,1)} %get-tuple-element.44.rows_ref, s32[32,128]{1,0:T(8,128)S(1)} %get-tuple-element.45.start_ref, s32[32,128]{1,0:T(8,128)S(1)} %get-tuple-element.46.end_ref, ...), custom_call_target="tpu_custom_call" | custom-call | tf_op jit(solution)/shard_map/cond/branch_1_fun/frames_near/pallas_call | solution.py:745
  58.9 0.0 copy-start.1
  58.9 0.9 %copy-done.1 = bf16[768,512]{1,0:T(8,128)(2,1)} copy-done((bf16[768,512]{1,0:T(8,128)(2,1)}, bf16[768,512]{1,0:T(8,128)(2,1)S(1)}, u32[]{:S(2)}) %copy-start.1) | copy-done | bytes 786456
Async XLA Ops:
  0.0 53.5 %copy-start = (bf16[5,512,512]{2,1,0:T(8,128)(2,1)S(1)}, bf16[5,512,512]{2,1,0:T(8,128)(2,1)}, u32[]{:S(2)}) copy-start(bf16[5,512,512]{2,1,0:T(8,128)(2,1)} %param.19) | copy-start | bytes 7864324
  0.0 53.5 %copy-start.2 = (f32[512]{0:T(512)S(1)}, f32[512]{0:T(512)}, u32[]{:S(2)}) copy-start(f32[512]{0:T(512)} %param.20) | copy-start | bytes 6148
  0.0 53.5 %copy-start.3 = (f32[512]{0:T(512)S(1)}, f32[512]{0:T(512)}, u32[]{:S(2)}) copy-start(f32[512]{0:T(512)} %param.21) | copy-start | bytes 6148
  58.9 0.9 %copy-start.1 = (bf16[768,512]{1,0:T(8,128)(2,1)}, bf16[768,512]{1,0:T(8,128)(2,1)S(1)}, u32[]{:S(2)}) copy-start(bf16[768,512]{1,0:T(8,128)(2,1)S(1)} %get-tuple-element.63) | copy-start | bytes 2359300

commit v5 on v4

--- a/solution.py
+++ b/solution.py
@@ -22,6 +22,7 @@
 STEPS = FRAMES // STEP
 TILE = 256
 BLOCKS = 8
+UNROLL = 2
 GROUPS = 8
 NEG = -1e30
 MIB = 1024 * 1024
@@ -92,16 +93,17 @@
     h_ref,
     meta_ref,
     wbuf,
-    send_kv,
-    send_q,
+    send_kq,
+    send_v,
     meta_all,
     flags,
-    kv_ref,
-    q_ref,
+    kq_ref,
+    k_ref,
+    v_ref,
     mark_ref,
     seg_ref,
-    even_ref,
-    odd_ref,
+    scores,
+    tops,
     send_o,
     landed,
     w_out,
@@ -109,12 +111,14 @@
     mine,
     w_sem,
     load_sem,
-    kv_send,
-    kv_recv,
-    q_send,
-    q_recv,
-    pass_send,
-    pass_recv,
+    kq_send,
+    kq_recv,
+    v_send,
+    v_recv,
+    pass_k_send,
+    pass_k_recv,
+    pass_v_send,
+    pass_v_recv,
     meta_send,
     meta_recv,
     flag_send,
@@ -151,10 +155,10 @@
         )
 
     for i in range(4):
+        w_copy(i, 0).start()
         w_copy(i, 1).start()
+    for i in range(4):
         w_copy(i, 2).start()
-    for i in range(4):
-        w_copy(i, 0).start()
     loads = [
         pltpu.make_async_copy(a, b, load_sem.at[i])
         for i, (a, b) in enumerate(((w_out_ref, w_out), (w_proj_ref, w_proj)))
@@ -194,82 +198,95 @@
         device_id_type=MESH,
     )
 
-    def kv_copy(head, source):
+    def kq_copy(head, source):
         return pltpu.make_async_remote_copy(
-            src_ref=send_kv.at[head],
-            dst_ref=kv_ref.at[2 * source + core],
-            send_sem=kv_send.at[head],
-            recv_sem=kv_recv.at[source],
+            src_ref=send_kq.at[head],
+            dst_ref=kq_ref.at[source],
+            send_sem=kq_send.at[head],
+            recv_sem=kq_recv.at[source],
             device_id=seq(2 * head + core),
             device_id_type=MESH,
         )
 
-    def q_copy(head, source):
+    def v_copy(head, source):
         return pltpu.make_async_remote_copy(
-            src_ref=send_q.at[head],
-            dst_ref=q_ref.at[source],
-            send_sem=q_send.at[head],
-            recv_sem=q_recv.at[source],
+            src_ref=send_v.at[head],
+            dst_ref=v_ref.at[source, core],
+            send_sem=v_send.at[head],
+            recv_sem=v_recv.at[source],
             device_id=seq(2 * head + core),
             device_id_type=MESH,
         )
 
-    own_kv = pltpu.make_async_copy(send_kv.at[chip], kv_ref.at[me], own_sem.at[0])
-    own_q = pltpu.make_async_copy(send_q.at[chip], q_ref.at[chip], own_sem.at[1])
-    own_pass = pltpu.make_async_remote_copy(
-        src_ref=send_kv.at[chip],
-        dst_ref=kv_ref.at[me],
-        send_sem=pass_send.at[chip],
-        recv_sem=pass_recv.at[chip],
-        device_id=seq(sibling),
-        device_id_type=MESH,
-    )
+    def pass_k(source, block):
+        return pltpu.make_async_remote_copy(
+            src_ref=block,
+            dst_ref=k_ref.at[source],
+            send_sem=pass_k_send.at[source],
+            recv_sem=pass_k_recv.at[source],
+            device_id=seq(sibling),
+            device_id_type=MESH,
+        )
+
+    def pass_v(source, block):
+        return pltpu.make_async_remote_copy(
+            src_ref=block,
+            dst_ref=v_ref.at[source, core],
+            send_sem=pass_v_send.at[source],
+            recv_sem=pass_v_recv.at[source],
+            device_id=seq(sibling),
+            device_id_type=MESH,
+        )
+
+    own_kq = pltpu.make_async_copy(send_kq.at[chip], kq_ref.at[chip], own_sem.at[0])
+    own_v = pltpu.make_async_copy(send_v.at[chip], v_ref.at[chip, core], own_sem.at[1])
 
     low = low_lanes(ROWS // 2)
     for i in range(4):
         g = group_at(own, i)
+        w_copy(i, 0).wait()
         w_copy(i, 1).wait()
-        w_copy(i, 2).wait()
         h = h_ref[...]
-        k4, v4 = (
-            jnp.dot(h, wbuf[i, t], preferred_element_type=jnp.float32) for t in (1, 2)
+        q4, k4 = (
+            jnp.dot(h, wbuf[i, t], preferred_element_type=jnp.float32) for t in (0, 1)
         )
         for j in range(2):
             at = slice(128 * j, 128 * j + 128)
-            v2 = jnp.transpose(v4[:, at]).astype(jnp.bfloat16)
+            q2 = jnp.transpose(q4[:, at] * 0.125).astype(jnp.bfloat16)
             k2 = k4[:, at]
             turned = pltpu.roll(k2, HEAD, 1)
             first = 4 * g + 2 * j
-            send_kv[first, 0] = jnp.where(low, k2[:64], turned[64:]).astype(jnp.bfloat16)
-            send_kv[first + 1, 0] = jnp.where(low, turned[:64], k2[64:]).astype(jnp.bfloat16)
-            send_kv[first, 1] = v2[:64]
-            send_kv[first + 1, 1] = v2[64:]
+            send_kq[first, 0] = jnp.where(low, k2[:64], turned[64:]).astype(jnp.bfloat16)
+            send_kq[first + 1, 0] = jnp.where(low, turned[:64], k2[64:]).astype(jnp.bfloat16)
+            send_kq[first, 1] = q2[:64]
+            send_kq[first + 1, 1] = q2[64:]
         if i == 0:
             beside = jnp.where(me > 0, 1, 0) + jnp.where(me < SEQ - 1, 1, 0)
             await_greetings(CHIPS - 1 + beside + GROUPS - 1)
         for r in range(4):
             if i == 3 and r == 0:
-                own_kv.start()
-                own_pass.start()
+                own_kq.start()
+                pass_k(chip, send_kq.at[chip, 0]).start()
             else:
-                kv_copy(4 * g + lax.rem(chip + r, 4), chip).start()
+                kq_copy(4 * g + lax.rem(chip + r, 4), chip).start()
         if i == 0:
             lax.fori_loop(1, CHIPS, send_meta, 0)
             own_meta.start()
     for i in range(4):
         g = group_at(own, i)
-        w_copy(i, 0).wait()
-        q4 = jnp.dot(h_ref[...], wbuf[i, 0], preferred_element_type=jnp.float32) * 0.125
+        w_copy(i, 2).wait()
+        v4 = jnp.dot(h_ref[...], wbuf[i, 2], preferred_element_type=jnp.float32)
         for j in range(2):
-            q2 = jnp.transpose(q4[:, 128 * j : 128 * j + 128]).astype(jnp.bfloat16)
+            v2 = jnp.transpose(v4[:, 128 * j : 128 * j + 128]).astype(jnp.bfloat16)
             first = 4 * g + 2 * j
-            send_q[first] = q2[:64]
-            send_q[first + 1] = q2[64:]
+            send_v[first] = v2[:64]
+            send_v[first + 1] = v2[64:]
         for r in range(4):
             if i == 3 and r == 0:
-                own_q.start()
+                own_v.start()
+                pass_v(chip, send_v.at[chip]).start()
             else:
-                q_copy(4 * g + lax.rem(chip + r, 4), chip).start()
+                v_copy(4 * g + lax.rem(chip + r, 4), chip).start()
 
     def await_meta(i, carry):
         meta_copy(i, lax.rem(chip + CHIPS - i, CHIPS)).wait()
@@ -355,34 +372,19 @@
         total = total + flags[i]
     far_ref[0, 0] = jnp.sum(total).astype(jnp.int32)
 
-    def passing(source):
-        return pltpu.make_async_remote_copy(
-            src_ref=kv_ref.at[2 * source + core],
-            dst_ref=kv_ref.at[2 * source + core],
-            send_sem=pass_send.at[source],
-            recv_sem=pass_recv.at[source],
-            device_id=seq(sibling),
-            device_id_type=MESH,
-        )
-
-    for i in range(4):
-        for r in range(4):
-            if i == 3 and r == 0:
-                continue
-            source = 4 * group_at(own, i) + lax.rem(chip + 4 - r, 4)
-            kv_copy(source, source).wait_recv()
-            passing(source).start()
-
-    for i in range(4):
-        for r in range(4):
-            source = 4 * group_at(own, i) + lax.rem(chip + 4 - r, 4)
-            if i == 3 and r == 0:
-                own_kv.wait()
-                own_q.wait()
-                own_pass.wait_recv()
-            else:
-                q_copy(source, source).wait_recv()
-                passing(source).wait_recv()
+    arrivals = [
+        4 * group_at(own, i) + lax.rem(chip + 4 - r, 4)
+        for i in range(4)
+        for r in range(4)
+        if i < 3 or r > 0
+    ]
+    for source in arrivals:
+        kq_copy(source, source).wait_recv()
+        pass_k(source, kq_ref.at[source, 0]).start()
+    own_kq.wait()
+    pass_k(chip, send_kq.at[chip, 0]).wait()
+    for source in arrivals:
+        pass_k(source, kq_ref.at[source, 0]).wait()
 
     pairs = CHIPS // 2
 
@@ -393,7 +395,7 @@
 
     def right_side(p):
         first = 4 * p + core
-        q = jnp.concatenate([q_ref[2 * p], q_ref[2 * p + 1]], axis=1)
+        q = jnp.concatenate([kq_ref[2 * p, 1], kq_ref[2 * p + 1, 1]], axis=1)
         zero = jnp.zeros((HEAD, 256), jnp.bfloat16)
         rows = lax.broadcasted_iota(jnp.int32, (8, 128), 0)
         bias = jnp.concatenate(
@@ -418,19 +420,18 @@
             axis=0,
         )
 
-    def score(right, block, keep, top):
-        left = jnp.concatenate(
-            [
-                jnp.concatenate([kv_ref[block + t, 0], mark_ref[block + t]], axis=1)
-                for t in range(BLOCKS)
-            ],
-            axis=0,
-        )
-        s = jnp.dot(left, right, preferred_element_type=jnp.float32)
+    def score(right, n, keep, top):
+        these = range(BLOCKS // 2 * n, BLOCKS // 2 * (n + 1))
+        rows = [
+            jnp.concatenate([kq_ref[c, 0], mark_ref[2 * c + core]], axis=1) for c in these
+        ] + [jnp.concatenate([k_ref[c], mark_ref[2 * c + 1 - core]], axis=1) for c in these]
+        s = jnp.dot(
+            jnp.concatenate(rows, axis=0), right, preferred_element_type=jnp.float32
+        )
         keep[...] = s
         return jnp.maximum(top, jnp.max(s.reshape(8 * BLOCKS, 8, 512), axis=0))
 
-    def collect(top, block, kept, acc):
+    def collect(top, n, kept, acc):
         w = jnp.exp(kept[...] - top).astype(jnp.bfloat16)
         w = jnp.concatenate(
             [
@@ -440,7 +441,10 @@
             ],
             axis=0,
         )
-        v = jnp.concatenate([kv_ref[block + t, 1] for t in range(BLOCKS)], axis=1)
+        these = range(BLOCKS // 2 * n, BLOCKS // 2 * (n + 1))
+        v = jnp.concatenate(
+            [v_ref[c, core] for c in these] + [v_ref[c, 1 - core] for c in these], axis=1
+        )
         v = jnp.concatenate([v, ones], axis=0)
         return acc + jnp.dot(v, w, preferred_element_type=jnp.float32)
 
@@ -478,30 +482,37 @@
     low = jnp.full((8, 512), NEG, jnp.float32)
     clear = jnp.zeros((HEAD + 16, 256), jnp.float32)
     chunks = SEQ // BLOCKS
-    right = right_side(pair_at(0))
-    top = low
-    for n in range(chunks):
-        top = score(right, BLOCKS * n, even_ref.at[n], top)
-
-    def both(i, here, there, top):
+    def score_pair(i):
         right = right_side(pair_at(i))
-        new_top, acc = low, clear
+        top = low
         for n in range(chunks):
-            new_top = score(right, BLOCKS * n, here.at[n], new_top)
-            acc = collect(top, BLOCKS * n, there.at[n], acc)
-        give(i - 1, acc)
-        return peak(new_top)
-
-    def two(i, top):
-        top = both(2 * i + 1, odd_ref, even_ref, top)
-        return both(2 * i + 2, even_ref, odd_ref, top)
-
-    top = lax.fori_loop(0, pairs // 2 - 1, two, peak(top))
-    top = both(pairs - 1, odd_ref, even_ref, top)
-    acc = clear
-    for n in range(chunks):
-        acc = collect(top, BLOCKS * n, odd_ref.at[n], acc)
-    give(pairs - 1, acc)
+            top = score(right, n, scores.at[i, n], top)
+        tops[i] = peak(top)
+
+    def collect_pair(i):
+        acc, top = clear, tops[i]
+        for n in range(chunks):
+            acc = collect(top, n, scores.at[i, n], acc)
+        return acc
+
+    for i in range(0, pairs, UNROLL):
+        for u in range(UNROLL):
+            score_pair(i + u)
+        for source in arrivals[2 * i : 2 * (i + UNROLL)]:
+            v_copy(source, source).wait_recv()
+            pass_v(source, v_ref.at[source, core]).start()
+    own_v.wait()
+    pass_v(chip, send_v.at[chip]).wait()
+    for source in arrivals:
+        pass_v(source, v_ref.at[source, core]).wait()
+
+    def some(i, carry):
+        accs = [collect_pair(UNROLL * i + u) for u in range(UNROLL)]
+        for u in range(UNROLL):
+            give(UNROLL * i + u, accs[u])
+        return carry
+
+    lax.fori_loop(0, pairs // UNROLL, some, 0)
 
     for load in loads:
         load.wait()
@@ -557,14 +568,9 @@
         return carry
 
     lax.fori_loop(1, CHIPS, sent, 0)
-    for i in range(4):
-        for r in range(4):
-            source = 4 * group_at(own, i) + lax.rem(chip + 4 - r, 4)
-            if i < 3 or r > 0:
-                q_copy(source, source).wait_send()
-                kv_copy(source, source).wait_send()
-                passing(source).wait_send()
-    own_pass.wait_send()
+    for source in arrivals:
+        kq_copy(source, source).wait_send()
+        v_copy(source, source).wait_send()
 
     for slot in range(3):
 
@@ -612,12 +618,13 @@
             pltpu.VMEM((HEADS,) + half, jnp.bfloat16),
             pltpu.VMEM((CHIPS, 2, 2, 128), jnp.int32),
             pltpu.VMEM((GROUPS, 8, 128), jnp.float32),
-            pltpu.VMEM((SEQ, 2) + half, jnp.bfloat16),
+            pltpu.VMEM((CHIPS, 2) + half, jnp.bfloat16),
             pltpu.VMEM((CHIPS,) + half, jnp.bfloat16),
+            pltpu.VMEM((CHIPS, 2) + half, jnp.bfloat16),
             pltpu.VMEM((SEQ,) + half, jnp.bfloat16),
             pltpu.VMEM((SEQ, 128), jnp.int32),
-            pltpu.VMEM((SEQ // BLOCKS, 64 * BLOCKS, 512), jnp.float32),
-            pltpu.VMEM((SEQ // BLOCKS, 64 * BLOCKS, 512), jnp.float32),
+            pltpu.VMEM((CHIPS // 2, SEQ // BLOCKS, 64 * BLOCKS, 512), jnp.float32),
+            pltpu.VMEM((CHIPS // 2, 1, 512), jnp.float32),
             pltpu.VMEM((CHIPS,) + half, jnp.bfloat16),
             pltpu.VMEM((CHIPS,) + half, jnp.bfloat16),
             pltpu.VMEM((WIDTH, WIDTH), jnp.bfloat16),
@@ -625,6 +632,8 @@
             pltpu.VMEM((ROWS, CHANNELS), jnp.bfloat16),
             dma((4, 3)),
             dma((2,)),
+            dma((HEADS,)),
+            dma((HEADS,)),
             dma((HEADS,)),
             dma((HEADS,)),
             dma((HEADS,)),
@@ -748,7 +757,7 @@
         in_specs=[pl.BlockSpec(memory_space=pltpu.SMEM)] + [vmem] * 6,
         out_specs=vmem,
         scratch_shapes=[pltpu.VMEM((FRAMES, KERNEL * CHANNELS), jnp.bfloat16)],
-        compiler_params=pltpu.CompilerParams(vmem_limit_bytes=60 * MIB),
+        compiler_params=pltpu.CompilerParams(vmem_limit_bytes=61 * MIB),
         name="frames_near" if near else "frames_far",
     )(ranges, rows, starts, ends, conv_w, conv_b, conv_gain)
 

time: 60.7 us -> 63.3 us (1.043); the launches traced: 59.8 us -> 63.2 us
  Pallas kernels: 58.1 us -> 62.2 us
  local copies, waits for them, and re-layouts: 0.89 us -> 0.01 us
    pallas_call x1, Pallas kernels: 52.9 us -> 56.6 us  [mix(): pl.pallas_call(mix_kernel, out_shape=(jax.ShapeDtypeStruct((3, ROWS, CHAN...]
    unnamed x8 -> x6, local copies, waits for them, and re-layouts: 0.89 us -> 0.01 us
where the time goes in v5:
time: 63.3 us; the launch traced here: 63.2 us
  Pallas kernels  62.2 us (98%)
  between operations  0.73 us (1%)
    pallas_call x1, Pallas kernels, mix(): pl.pallas_call(mix_kernel, out_shape=(jax.ShapeDtypeStruct((3, ROWS, CHAN...  56.6 us
    pallas_call x1, Pallas kernels, frames(): pl.pallas_call(functools.partial(frames_kernel, near), out_shape=jax.Shap...  5.63 us

profile of v5, /device:TPU:1, one launch (start us, length us, event | category | flops | bytes accessed | tf_op | source)
XLA Modules:
  0.0 63.2 jit_solution(293119950084980877)
XLA Ops:
  0.0 0.0 copy-start
  0.0 0.0 copy-start.1
  0.0 0.0 copy-start.2
  0.0 56.6 %mix.1 = (bf16[3,128,512]{2,1,0:T(8,128)(2,1)S(1)}, s32[32,128]{1,0:T(8,128)S(1)}, s32[32,128]{1,0:T(8,128)S(1)}, s32[8,128]{1,0:T(8,128)S(1)}, s32[1,1]{1,0:T(1,128)}) custom-call(bf16[128,1024]{1,0:T(8,128)(2,1)} %units_ref.1, f32[1,1024]{1,0:T(1,128)} %bitcast.15, s32[1,128]{1,0:T(1,128)} %bitcast.16, s32[1,128]{1,0:T(1,128)} %bitcast.17, ...), custom_call_target="tpu_custom_call" | custom-call | tf_op jit(solution)/shard_map/mix/pallas_call | solution.py:602
  57.3 0.0 copy-done
  57.3 0.0 copy-done.1
  57.3 0.0 copy-done.2
  57.4 5.8 %conditional.1 = (bf16[768,512]{1,0:T(8,128)(2,1)}) conditional(s32[]{:T(128)} %bitcast.4, (bf16[3,128,512]{2,1,0:T(8,128)(2,1)S(1)}, s32[8,128]{1,0:T(8,128)S(1)}, s32[32,128]{1,0:T(8,128)S(1)}, s32[32,128]{1,0:T(8,128)S(1)}, bf16[2560,512]{1,0:T(8,128)(2,1)S(1)}, /*index=5*/f32[1,512]{1,0:T(1,128)S(1)}, f32[1,512]{1,0:T(1,128)S(1)}) %tuple.21, ...), branch_computations={%region_0.1_spmd, %region_1.2_spmd} | conditional | flops 10 | bytes 262270 | solution.py:785
  57.6 5.6 %frames_near.1 = bf16[768,512]{1,0:T(8,128)(2,1)} custom-call(s32[8,128]{1,0:T(8,128)S(1)} %get-tuple-element.43.range_ref, bf16[3,128,512]{2,1,0:T(8,128)(2,1)S(1)} %get-tuple-element.44.rows_ref, s32[32,128]{1,0:T(8,128)S(1)} %get-tuple-element.45.start_ref, s32[32,128]{1,0:T(8,128)S(1)} %get-tuple-element.46.end_ref, ...), custom_call_target="tpu_custom_call" | custom-call | tf_op jit(solution)/shard_map/cond/branch_1_fun/frames_near/pallas_call | solution.py:754
Async XLA Ops:
  0.0 57.3 %copy-start = (bf16[5,512,512]{2,1,0:T(8,128)(2,1)S(1)}, bf16[5,512,512]{2,1,0:T(8,128)(2,1)}, u32[]{:S(2)}) copy-start(bf16[5,512,512]{2,1,0:T(8,128)(2,1)} %param.19) | copy-start | bytes 7864324
  0.0 57.3 %copy-start.1 = (f32[512]{0:T(512)S(1)}, f32[512]{0:T(512)}, u32[]{:S(2)}) copy-start(f32[512]{0:T(512)} %param.20) | copy-start | bytes 6148
  0.0 57.3 %copy-start.2 = (f32[512]{0:T(512)S(1)}, f32[512]{0:T(512)}, u32[]{:S(2)}) copy-start(f32[512]{0:T(512)} %param.21) | copy-start | bytes 6148

commit v6 on v4

--- a/solution.py
+++ b/solution.py
@@ -131,19 +131,6 @@
     chip = me // 2
     sibling = me + 1 - 2 * core
     own = chip // 4
-    greet_row(me)
-    for there in (-1, 1):
-
-        @pl.when((me + there >= 0) & (me + there < SEQ))
-        def _():
-            greet(seq(lax.rem(me + SEQ + there, SEQ)))
-
-    def greet_part(i, carry):
-        greet({"grp": lax.rem(part + i, GROUPS)})
-        return carry
-
-    lax.fori_loop(1, GROUPS, greet_part, 0)
-
     def w_copy(i, t):
         g = group_at(own, i)
         return pltpu.make_async_copy(
@@ -153,6 +140,19 @@
     for i in range(4):
         w_copy(i, 1).start()
         w_copy(i, 2).start()
+    greet_row(me)
+    for there in (-1, 1):
+
+        @pl.when((me + there >= 0) & (me + there < SEQ))
+        def _():
+            greet(seq(lax.rem(me + SEQ + there, SEQ)))
+
+    def greet_part(i, carry):
+        greet({"grp": lax.rem(part + i, GROUPS)})
+        return carry
+
+    lax.fori_loop(1, GROUPS, greet_part, 0)
+
     for i in range(4):
         w_copy(i, 0).start()
     loads = [
@@ -265,11 +265,15 @@
             first = 4 * g + 2 * j
             send_q[first] = q2[:64]
             send_q[first + 1] = q2[64:]
-        for r in range(4):
-            if i == 3 and r == 0:
-                own_q.start()
-            else:
-                q_copy(4 * g + lax.rem(chip + r, 4), chip).start()
+
+    own_q.start()
+    beside_chip = chip + 1 - 2 * lax.rem(chip, 2)
+    pairs = CHIPS // 2
+    q_targets = [beside_chip] + [
+        2 * lax.rem(chip // 2 + pairs - i, pairs) + e for i in range(1, pairs) for e in range(2)
+    ]
+    for target in q_targets:
+        q_copy(target, chip).start()
 
     def await_meta(i, carry):
         meta_copy(i, lax.rem(chip + CHIPS - i, CHIPS)).wait()
@@ -365,26 +369,21 @@
             device_id_type=MESH,
         )
 
-    for i in range(4):
-        for r in range(4):
-            if i == 3 and r == 0:
-                continue
-            source = 4 * group_at(own, i) + lax.rem(chip + 4 - r, 4)
-            kv_copy(source, source).wait_recv()
-            passing(source).start()
-
-    for i in range(4):
-        for r in range(4):
-            source = 4 * group_at(own, i) + lax.rem(chip + 4 - r, 4)
-            if i == 3 and r == 0:
-                own_kv.wait()
-                own_q.wait()
-                own_pass.wait_recv()
-            else:
-                q_copy(source, source).wait_recv()
-                passing(source).wait_recv()
-
-    pairs = CHIPS // 2
+    arrivals = [
+        4 * group_at(own, i) + lax.rem(chip + 4 - r, 4)
+        for i in range(4)
+        for r in range(4)
+        if i < 3 or r > 0
+    ]
+    for j, source in enumerate(arrivals):
+        kv_copy(source, source).wait_recv()
+        passing(source).start()
+
+    own_kv.wait()
+    own_pass.wait_recv()
+    for source in arrivals:
+        passing(source).wait_recv()
+
 
     def pair_at(i):
         return lax.rem(chip // 2 + i, pairs)
@@ -478,12 +477,17 @@
     low = jnp.full((8, 512), NEG, jnp.float32)
     clear = jnp.zeros((HEAD + 16, 256), jnp.float32)
     chunks = SEQ // BLOCKS
+    own_q.wait()
+    q_copy(beside_chip, beside_chip).wait_recv()
     right = right_side(pair_at(0))
     top = low
     for n in range(chunks):
         top = score(right, BLOCKS * n, even_ref.at[n], top)
 
     def both(i, here, there, top):
+        for e in range(2):
+            source = 2 * pair_at(i) + e
+            q_copy(source, source).wait_recv()
         right = right_side(pair_at(i))
         new_top, acc = low, clear
         for n in range(chunks):
@@ -506,20 +510,19 @@
     for load in loads:
         load.wait()
 
-    def receive(i, carry):
-        o_copy(chip, lax.rem(chip + CHIPS - i, CHIPS)).wait_recv()
-        return carry
-
-    own_o.wait()
-    lax.fori_loop(1, CHIPS, receive, 0)
-    turned = [
-        jnp.transpose(
-            jnp.concatenate([landed[2 * j], landed[2 * j + 1]], axis=0).astype(jnp.float32)
-        ).astype(jnp.bfloat16)
-        for j in range(HEADS // 2)
-    ]
-    attended = jnp.concatenate(turned, axis=1)
-    mixed = jnp.dot(attended, w_out[...], preferred_element_type=jnp.float32)
+    mixed = jnp.zeros((ROWS, WIDTH), jnp.float32)
+    for i in range(pairs):
+        p = lax.rem(chip // 2 + pairs - i, pairs)
+        if i == 0:
+            own_o.wait()
+            o_copy(chip, beside_chip).wait_recv()
+        else:
+            for e in range(2):
+                o_copy(chip, 2 * p + e).wait_recv()
+        heads = landed[pl.ds(2 * p, 2)].reshape(128, 128)
+        turned = jnp.transpose(heads.astype(jnp.float32)).astype(jnp.bfloat16)
+        rows = w_out[pl.ds(pl.multiple_of(128 * p, 128), 128), :]
+        mixed = mixed + jnp.dot(turned, rows, preferred_element_type=jnp.float32)
     mixed = (mixed + units_ref[...].astype(jnp.float32)).astype(jnp.bfloat16)
     mine[...] = jnp.dot(mixed, w_proj[...], preferred_element_type=jnp.float32).astype(
         jnp.bfloat16
@@ -557,13 +560,10 @@
         return carry
 
     lax.fori_loop(1, CHIPS, sent, 0)
-    for i in range(4):
-        for r in range(4):
-            source = 4 * group_at(own, i) + lax.rem(chip + 4 - r, 4)
-            if i < 3 or r > 0:
-                q_copy(source, source).wait_send()
-                kv_copy(source, source).wait_send()
-                passing(source).wait_send()
+    for source in arrivals:
+        q_copy(source, source).wait_send()
+        kv_copy(source, source).wait_send()
+        passing(source).wait_send()
     own_pass.wait_send()
 
     for slot in range(3):
@@ -663,14 +663,18 @@
         frame = lax.broadcasted_iota(jnp.int32, (STEP, 256), 0)
         first = FRAMES * me + STEP * f - KERNEL // 2
         starts, ends = starts - first, ends - first
+        chosen = jnp.concatenate(
+            [
+                jnp.where((frame >= starts - j) & (frame < ends - j), 1.0, 0.0).astype(jnp.bfloat16)
+                for j in range(KERNEL)
+            ],
+            axis=0,
+        )
+        rows = jnp.dot(chosen, window, preferred_element_type=jnp.float32).astype(jnp.bfloat16)
         for j in range(KERNEL):
-            chosen = jnp.where((frame >= starts - j) & (frame < ends - j), 1.0, 0.0)
-            rows = jnp.dot(
-                chosen.astype(jnp.bfloat16), window, preferred_element_type=jnp.float32
-            )
-            stacked[STEP * f : STEP * f + STEP, CHANNELS * j : CHANNELS * j + CHANNELS] = (
-                rows.astype(jnp.bfloat16)
-            )
+            stacked[STEP * f : STEP * f + STEP, CHANNELS * j : CHANNELS * j + CHANNELS] = rows[
+                STEP * j : STEP * j + STEP
+            ]
     bias, gain = b_ref[...], gain_ref[...]
     for r in range(FRAMES // TILE):
         at = slice(TILE * r, TILE * r + TILE)
@@ -748,7 +752,7 @@
         in_specs=[pl.BlockSpec(memory_space=pltpu.SMEM)] + [vmem] * 6,
         out_specs=vmem,
         scratch_shapes=[pltpu.VMEM((FRAMES, KERNEL * CHANNELS), jnp.bfloat16)],
-        compiler_params=pltpu.CompilerParams(vmem_limit_bytes=60 * MIB),
+        compiler_params=pltpu.CompilerParams(vmem_limit_bytes=61 * MIB),
         name="frames_near" if near else "frames_far",
     )(ranges, rows, starts, ends, conv_w, conv_b, conv_gain)
 

time: 60.7 us -> 59.3 us (0.977)
  local copies, waits for them, and re-layouts: 0.89 us -> 0.01 us
    unnamed x8 -> x6, local copies, waits for them, and re-layouts: 0.89 us -> 0.01 us
where the time goes in v6:
time: 59.3 us; the launch traced here: 58.8 us
  Pallas kernels  57.9 us (98%)
  between operations  0.73 us (1%)
    pallas_call x1, Pallas kernels, mix(): pl.pallas_call(mix_kernel, out_shape=(jax.ShapeDtypeStruct((3, ROWS, CHAN...  52.8 us
    pallas_call x1, Pallas kernels, frames(): pl.pallas_call(functools.partial(frames_kernel, near), out_shape=jax.Shap...  5.01 us

profile of v6, /device:TPU:1, one launch (start us, length us, event | category | flops | bytes accessed | tf_op | source)
XLA Modules:
  0.0 58.8 jit_solution(6382604609834112325)
XLA Ops:
  0.0 0.0 copy-start
  0.0 0.0 copy-start.1
  0.0 0.0 copy-start.2
  0.0 52.8 %mix.1 = (bf16[3,128,512]{2,1,0:T(8,128)(2,1)S(1)}, s32[32,128]{1,0:T(8,128)S(1)}, s32[32,128]{1,0:T(8,128)S(1)}, s32[8,128]{1,0:T(8,128)S(1)}, s32[1,1]{1,0:T(1,128)}) custom-call(bf16[128,1024]{1,0:T(8,128)(2,1)} %units_ref.1, f32[1,1024]{1,0:T(1,128)} %bitcast.15, s32[1,128]{1,0:T(1,128)} %bitcast.16, s32[1,128]{1,0:T(1,128)} %bitcast.17, ...), custom_call_target="tpu_custom_call" | custom-call | tf_op jit(solution)/shard_map/mix/pallas_call | solution.py:596
  53.6 0.0 copy-done
  53.6 0.0 copy-done.1
  53.6 0.0 copy-done.2
  53.6 5.2 %conditional.1 = (bf16[768,512]{1,0:T(8,128)(2,1)}) conditional(s32[]{:T(128)} %bitcast.4, (bf16[3,128,512]{2,1,0:T(8,128)(2,1)S(1)}, s32[8,128]{1,0:T(8,128)S(1)}, s32[32,128]{1,0:T(8,128)S(1)}, s32[32,128]{1,0:T(8,128)S(1)}, bf16[2560,512]{1,0:T(8,128)(2,1)S(1)}, /*index=5*/f32[1,512]{1,0:T(1,128)S(1)}, f32[1,512]{1,0:T(1,128)S(1)}) %tuple.21, ...), branch_computations={%region_0.1_spmd, %region_1.2_spmd} | conditional | flops 10 | bytes 262270 | solution.py:780
  53.8 5.0 %frames_near.1 = bf16[768,512]{1,0:T(8,128)(2,1)} custom-call(s32[8,128]{1,0:T(8,128)S(1)} %get-tuple-element.43.range_ref, bf16[3,128,512]{2,1,0:T(8,128)(2,1)S(1)} %get-tuple-element.44.rows_ref, s32[32,128]{1,0:T(8,128)S(1)} %get-tuple-element.45.start_ref, s32[32,128]{1,0:T(8,128)S(1)} %get-tuple-element.46.end_ref, ...), custom_call_target="tpu_custom_call" | custom-call | tf_op jit(solution)/shard_map/cond/branch_1_fun/frames_near/pallas_call | solution.py:749
Async XLA Ops:
  0.0 53.6 %copy-start = (bf16[5,512,512]{2,1,0:T(8,128)(2,1)S(1)}, bf16[5,512,512]{2,1,0:T(8,128)(2,1)}, u32[]{:S(2)}) copy-start(bf16[5,512,512]{2,1,0:T(8,128)(2,1)} %param.19) | copy-start | bytes 7864324
  0.0 53.6 %copy-start.1 = (f32[512]{0:T(512)S(1)}, f32[512]{0:T(512)}, u32[]{:S(2)}) copy-start(f32[512]{0:T(512)} %param.20) | copy-start | bytes 6148
  0.0 53.6 %copy-start.2 = (f32[512]{0:T(512)S(1)}, f32[512]{0:T(512)}, u32[]{:S(2)}) copy-start(f32[512]{0:T(512)} %param.21) | copy-start | bytes 6148
